TPU v7x, 32 devices: a whole 2x2x4 slice. The times are simulated.
32 devices in a mesh: xb: 8 (over z, y), yb: 4 (over x, core).
Axes of the slice: x: 2, y: 2, z: 4, core: 2. Of those that a mesh axis runs over, the one named last changes fastest.
Arguments:
- initial_guess: float32 [64, 256, 256], P('xb', 'yb'), may hold values from -4 to 4
- right_side: float32 [64, 256, 256], P('xb', 'yb'), may hold values from -8 to 8
- coefficient: float32 [64, 256, 256], P('xb', 'yb'), may hold values from 0.3 to 3
Outputs:
- fine_field: float32 [64, 256, 256], P('xb', 'yb')
- middle_field: float32 [32, 128, 128], P('xb', 'yb')
- lower_field: float32 [16, 64, 64], P('xb', 'yb')
- coarse_field: float32 [8, 32, 32], P('xb', 'yb')
All inputs are finite; a program needn't handle non-finite values.
Results may differ from a plain program's by a relative error of at most 0.00002.
Values sent between devices are 32-bit elements; how exact they have to be, the bound alone decides.
A program may use at most 192 MiB of HBM per device.

v0:
```python
import jax
import jax.numpy as jnp
from jax import lax
from jax.sharding import PartitionSpec as P

COARSE_ITERS = 8


damping_alpha = 0.05
cheb_theta = 1.15
cheb_delta = 0.85
cheb_sigma = cheb_theta / cheb_delta
cheb_first = 1.0 / cheb_sigma
cheb_second = 1.0 / (2.0 * cheb_sigma - cheb_first)
cheb_carry = cheb_second * cheb_first
cheb_resid = 2.0 * cheb_second / cheb_delta
jacobi_weight = 0.8


def with_halo(block, sides, width):
    for axis, dim in sides:
        count = lax.axis_size(axis)
        forward = [(i, i + 1) for i in range(count - 1)]
        backward = [(target, source) for source, target in forward]
        low = lax.ppermute(
            lax.slice_in_dim(block, block.shape[dim] - width, None, axis=dim), axis, forward
        )
        high = lax.ppermute(lax.slice_in_dim(block, 0, width, axis=dim), axis, backward)
        block = jnp.concatenate([low, block, high], axis=dim)
    return block


def neighbours(padded):
    return [
        padded[2:, 1:-1, 1:-1],
        padded[:-2, 1:-1, 1:-1],
        padded[1:-1, 2:, 1:-1],
        padded[1:-1, :-2, 1:-1],
        padded[1:-1, 1:-1, 2:],
        padded[1:-1, 1:-1, :-2],
    ]


def face_weights(padded_coef, scale):
    centre = padded_coef[1:-1, 1:-1, 1:-1]
    weights = [0.5 * scale * (centre + other) for other in neighbours(padded_coef)]
    diagonal = damping_alpha + weights[0]
    for other in weights[1:]:
        diagonal = diagonal + other
    return (weights, diagonal)


def apply_operator(padded, field, weights, diagonal):
    result = diagonal * field
    for weight, other in zip(weights, neighbours(padded)):
        result = result - weight * other
    return result


def smooth_level(start, right_side, coefficient, scale, extend, padded_coef=None):
    padded_coef = extend(coefficient)
    weights, diagonal = face_weights(padded_coef, scale)
    if start is None:
        start = jnp.zeros_like(right_side)
        residual = right_side
    else:
        residual = right_side - apply_operator(extend(start), start, weights, diagonal)
    first_step = residual / (cheb_theta * diagonal)
    first = start + first_step
    residual = right_side - apply_operator(extend(first), first, weights, diagonal)
    second_step = cheb_carry * first_step + cheb_resid * residual / diagonal
    second = first + second_step
    residual = right_side - apply_operator(extend(second), second, weights, diagonal)
    return (second, residual)


def restrict_field(field):
    sx, sy, sz = field.shape
    return field.reshape(sx // 2, 2, sy // 2, 2, sz // 2, 2).sum(axis=(1, 3, 5)) * 0.125


def coarse_solve(right_side, coefficient, scale, extend):
    weights, diagonal = face_weights(extend(coefficient), scale)
    field = jnp.zeros_like(right_side)
    for repeat in range(COARSE_ITERS):
        field = (
            field
            + jacobi_weight
            * (right_side - apply_operator(extend(field), field, weights, diagonal))
            / diagonal
        )
    leftover = right_side - apply_operator(extend(field), field, weights, diagonal)
    ones_field = jnp.ones_like(right_side)
    image_ones = apply_operator(extend(ones_field), ones_field, weights, diagonal)
    return field + jnp.sum(leftover) / jnp.sum(image_ones)


def extend_all(field):
    return jnp.pad(field, 1)


def extend_local(field):
    padded = with_halo(field, (("xb", 0), ("yb", 1)), 1)
    return jnp.pad(padded, ((0, 0), (0, 0), (1, 1)))


def collect_grid(right_side, coefficient):
    sx, sy, sz = right_side.shape
    count_x = lax.axis_size("xb")
    count_y = lax.axis_size("yb")
    flat = (
        lax.all_gather(right_side.reshape(1, -1), ("xb", "yb"), axis=0, tiled=True),
        lax.all_gather(coefficient.reshape(1, -1), ("xb", "yb"), axis=0, tiled=True),
    )
    return tuple(
        (
            piece.reshape(count_x, count_y, sx, sy, sz)
            .transpose(0, 2, 1, 3, 4)
            .reshape(count_x * sx, count_y * sy, sz)
            for piece in flat
        )
    )


def own_block(whole, shape):
    start_x = lax.axis_index("xb") * shape[0]
    start_y = lax.axis_index("yb") * shape[1]
    return lax.dynamic_slice(whole, (start_x, start_y, jnp.int32(0)), shape)


def per_device(initial_guess, right_side, coefficient):
    fine, fine_res = smooth_level(initial_guess, right_side, coefficient, 1.0, extend_local, None)
    mid_coef = restrict_field(coefficient)
    middle, mid_res = smooth_level(
        None, restrict_field(fine_res), mid_coef, 0.25, extend_local, None
    )
    low_coef = restrict_field(mid_coef)
    low_rhs = restrict_field(mid_res)
    lower, low_res = smooth_level(None, low_rhs, low_coef, 0.0625, extend_local, None)
    coarse_rhs, coarse_coef = collect_grid(restrict_field(low_res), restrict_field(low_coef))
    coarse_whole = coarse_solve(coarse_rhs, coarse_coef, 0.015625, extend_all)
    sx, sy, sz = right_side.shape
    coarse = own_block(coarse_whole, (sx // 8, sy // 8, sz // 8))
    return (fine, middle, lower, coarse)


def solution(mesh):
    placed = (P("xb", "yb", None), P("xb", "yb", None), P("xb", "yb", None))
    return jax.shard_map(
        per_device,
        mesh=mesh,
        in_specs=placed,
        out_specs=(
            P("xb", "yb", None),
            P("xb", "yb", None),
            P("xb", "yb", None),
            P("xb", "yb", None),
        ),
        check_vma=False,
    )
```

profile of v0, /device:TPU:0, one launch (start us, length us, event | category | flops | bytes accessed | tf_op | source)
XLA Modules:
  0.0 345.4 jit_solution(12159437463748348136)
XLA Ops:
  0.6 0.9 fusion.305
  1.5 4.9 %collective-permute-start.1 = (f32[1,64,256]{2,1,0:T(8,128)S(1)}, f32[1,64,256]{2,1,0:T(8,128)S(1)}, u32[]{:S(2)}, u32[]{:S(2)}) collective-permute-start(f32[1,64,256]{2,1,0:T(8,128)S(1)} %get-tuple-element.31), channel_id=1, source_target_pairs={{0,4},{4,8},{8,12},{12,16},{16,20},{20,24},{24,28},{1,5},{5,9},{9,... | collective-permute-start | bytes 196616 | tf_op jit(solution)/shard_map/ppermute | solution.py:25
  6.4 1.3 collective-permute-start
  7.7 0.9 fusion.306
  8.6 4.5 %collective-permute-start.5 = (f32[1,64,256]{2,1,0:T(8,128)S(1)}, f32[1,64,256]{2,1,0:T(8,128)S(1)}, u32[]{:S(2)}, u32[]{:S(2)}) collective-permute-start(f32[1,64,256]{2,1,0:T(8,128)S(1)} %get-tuple-element.33), channel_id=1, source_target_pairs={{0,4},{4,8},{8,12},{12,16},{16,20},{20,24},{24,28},{1,5},{5,9},{9,... | collective-permute-start | bytes 196616 | tf_op jit(solution)/shard_map/ppermute | solution.py:25
  13.1 1.3 collective-permute-start.4
  14.4 35.6 %reshape.61 = f32[4,2,32,2,128,2]{5,4,3,2,1,0:T(8,128)} reshape(f32[8,64,256]{2,1,0:T(8,128)} %param.5) | data formatting | bytes 1048576 | tf_op jit(solution)/shard_map/reshape | solution.py:79
  50.1 12.9 %reduce_sum.87 = f32[4,32,128]{2,1,0:T(8,128)} reduce(f32[4,2,32,2,128,2]{5,4,3,2,1,0:T(8,128)} %reshape.61, f32[]{:T(128)} %constant.19.clone.1), dimensions={1,3,5}, to_apply=%region_1.2 | reduce | flops 114688 | bytes 589828 | tf_op jit(solution)/shard_map/reduce_sum | solution.py:79
  63.1 1.4 collective-permute-start.2
  64.5 3.0 collective-permute-start.3
  67.7 1.3 collective-permute-start.6
  69.0 3.6 %collective-permute-start.7 = (f32[10,1,256]{2,1,0:T(1,128)S(1)}, f32[10,1,256]{2,1,0:T(1,128)S(1)}, u32[]{:S(2)}, u32[]{:S(2)}) collective-permute-start(f32[10,1,256]{2,1,0:T(1,128)S(1)} %get-tuple-element.24), channel_id=1, source_target_pairs={{0,1},{1,2},{2,3},{4,5},{5,6},{6,7},{8,9},{9,10},{10,11},{12,13},{... | collective-permute-start | bytes 30728 | tf_op jit(solution)/shard_map/ppermute | solution.py:25
  74.2 2.0 fusion.299
  76.2 1.3 collective-permute-start.8
  77.5 5.6 %collective-permute-start.9 = (f32[1,64,256]{2,1,0:T(8,128)S(1)}, f32[1,64,256]{2,1,0:T(8,128)S(1)}, u32[]{:S(2)}, u32[]{:S(2)}) collective-permute-start(f32[1,64,256]{2,1,0:T(8,128)S(1)} %get-tuple-element.28), channel_id=1, source_target_pairs={{0,4},{4,8},{8,12},{12,16},{16,20},{20,24},{24,28},{1,5},{5,9},{9,... | collective-permute-start | bytes 196616 | tf_op jit(solution)/shard_map/ppermute | solution.py:25
  83.4 2.7 collective-permute-done.9
  86.2 1.3 collective-permute-start.10
  87.5 3.0 collective-permute-start.11
  91.2 1.3 collective-permute-start.16
  92.4 5.6 %collective-permute-start.17 = (f32[1,32,128]{2,1,0:T(8,128)}, f32[1,32,128]{2,1,0:T(8,128)}, u32[]{:S(2)}, u32[]{:S(2)}) collective-permute-start(f32[1,32,128]{2,1,0:T(8,128)} %get-tuple-element.44), channel_id=1, source_target_pairs={{0,4},{4,8},{8,12},{12,16},{16,20},{20,24},{24,28},{1,5},{5,9},{9,... | collective-permute-start | bytes 49160 | tf_op jit(solution)/shard_map/ppermute | solution.py:25
  98.1 5.5 %mul.617 = f32[2,2,16,2,64,2]{5,4,3,2,1,0:T(8,128)} reshape(f32[4,32,128]{2,1,0:T(8,128)S(1)} %broadcast_multiply_fusion) | data formatting | bytes 131072 | tf_op jit(solution)/shard_map/mul | solution.py:79
  103.6 2.5 reduce_sum.89
  107.4 2.1 fusion.17
  109.5 1.3 collective-permute-start.12
  110.8 4.9 %collective-permute-start.13 = (f32[1,64,256]{2,1,0:T(8,128)S(1)}, f32[1,64,256]{2,1,0:T(8,128)S(1)}, u32[]{:S(2)}, u32[]{:S(2)}) collective-permute-start(f32[1,64,256]{2,1,0:T(8,128)S(1)} %get-tuple-element.26), channel_id=1, source_target_pairs={{0,4},{4,8},{8,12},{12,16},{16,20},{20,24},{24,28},{1,5},{5,9},{9,... | collective-permute-start | bytes 196616 | tf_op jit(solution)/shard_map/ppermute | solution.py:25
  116.4 1.3 collective-permute-start.18
  117.7 4.9 %collective-permute-start.19 = (f32[6,1,128]{2,1,0:T(1,128)S(1)}, f32[6,1,128]{2,1,0:T(1,128)S(1)}, u32[]{:S(2)}, u32[]{:S(2)}) collective-permute-start(f32[6,1,128]{2,1,0:T(1,128)S(1)} %get-tuple-element.38), channel_id=1, source_target_pairs={{0,1},{1,2},{2,3},{4,5},{5,6},{6,7},{8,9},{9,10},{10,11},{12,13},{... | collective-permute-start | bytes 9224 | tf_op jit(solution)/shard_map/ppermute | solution.py:25
  122.6 1.3 collective-permute-start.14
  123.9 4.5 %collective-permute-start.15 = (f32[10,1,256]{2,1,0:T(1,128)S(1)}, f32[10,1,256]{2,1,0:T(1,128)S(1)}, u32[]{:S(2)}, u32[]{:S(2)}) collective-permute-start(f32[10,1,256]{2,1,0:T(1,128)S(1)} %get-tuple-element.18), channel_id=1, source_target_pairs={{0,1},{1,2},{2,3},{4,5},{5,6},{6,7},{8,9},{9,10},{10,11},{12,13},{... | collective-permute-start | bytes 30728 | tf_op jit(solution)/shard_map/ppermute | solution.py:25
  128.4 1.6 select_maximum_fusion.20
  130.5 1.1 fusion.2
  131.6 34.9 %reshape.60 = f32[4,2,32,2,128,2]{5,4,3,2,1,0:T(8,128)} reshape(f32[8,64,256]{2,1,0:T(8,128)S(1)} %fusion.2) | data formatting | bytes 1048576 | tf_op jit(solution)/shard_map/reshape | solution.py:79
  166.5 12.3 %reduce_sum.86 = f32[4,32,128]{2,1,0:T(8,128)S(1)} reduce(f32[4,2,32,2,128,2]{5,4,3,2,1,0:T(8,128)} %reshape.60, f32[]{:T(128)} %constant.19.clone.1), dimensions={1,3,5}, to_apply=%region_0.1 | reduce | flops 114688 | bytes 589828 | tf_op jit(solution)/shard_map/reduce_sum | solution.py:79
  178.8 0.8 multiply_divide_fusion
  179.7 1.3 collective-permute-start.20
  181.0 5.2 %collective-permute-start.21 = (f32[1,32,128]{2,1,0:T(8,128)S(1)}, f32[1,32,128]{2,1,0:T(8,128)S(1)}, u32[]{:S(2)}, u32[]{:S(2)}) collective-permute-start(f32[1,32,128]{2,1,0:T(8,128)S(1)} %get-tuple-element.42), channel_id=1, source_target_pairs={{0,4},{4,8},{8,12},{12,16},{16,20},{20,24},{24,28},{1,5},{5,9},{9,... | collective-permute-start | bytes 49160 | tf_op jit(solution)/shard_map/ppermute | solution.py:25
  186.2 1.4 collective-permute-done.21
  187.6 1.3 collective-permute-start.22
  188.9 3.4 collective-permute-start.23
  192.3 1.3 collective-permute-start.28
  193.6 5.2 %collective-permute-start.29 = (f32[1,16,64]{2,1,0:T(8,128)S(1)}, f32[1,16,64]{2,1,0:T(8,128)S(1)}, u32[]{:S(2)}, u32[]{:S(2)}) collective-permute-start(f32[1,16,64]{2,1,0:T(8,128)S(1)} %get-tuple-element.57), channel_id=1, source_target_pairs={{0,4},{4,8},{8,12},{12,16},{16,20},{20,24},{24,28},{1,5},{5,9},{9,... | collective-permute-start | bytes 12296 | tf_op jit(solution)/shard_map/ppermute | solution.py:25
  199.0 0.9 fusion.232
  199.9 1.3 collective-permute-start.24
  201.2 5.6 %collective-permute-start.25 = (f32[1,32,128]{2,1,0:T(8,128)S(1)}, f32[1,32,128]{2,1,0:T(8,128)S(1)}, u32[]{:S(2)}, u32[]{:S(2)}) collective-permute-start(f32[1,32,128]{2,1,0:T(8,128)S(1)} %get-tuple-element.40), channel_id=1, source_target_pairs={{0,4},{4,8},{8,12},{12,16},{16,20},{20,24},{24,28},{1,5},{5,9},{9,... | collective-permute-start | bytes 49160 | tf_op jit(solution)/shard_map/ppermute | solution.py:25
  206.9 1.3 collective-permute-start.30
  208.2 4.5 %collective-permute-start.31 = (f32[4,1,64]{2,1,0:T(1,128)S(1)}, f32[4,1,64]{2,1,0:T(1,128)S(1)}, u32[]{:S(2)}, u32[]{:S(2)}) collective-permute-start(f32[4,1,64]{2,1,0:T(1,128)S(1)} %get-tuple-element.50), channel_id=1, source_target_pairs={{0,1},{1,2},{2,3},{4,5},{5,6},{6,7},{8,9},{9,10},{10,11},{12,13},{... | collective-permute-start | bytes 3080 | tf_op jit(solution)/shard_map/ppermute | solution.py:25
  212.7 1.3 collective-permute-start.26
  214.0 4.3 %collective-permute-start.27 = (f32[6,1,128]{2,1,0:T(1,128)S(1)}, f32[6,1,128]{2,1,0:T(1,128)S(1)}, u32[]{:S(2)}, u32[]{:S(2)}) collective-permute-start(f32[6,1,128]{2,1,0:T(1,128)S(1)} %get-tuple-element.34), channel_id=1, source_target_pairs={{0,1},{1,2},{2,3},{4,5},{5,6},{6,7},{8,9},{9,10},{10,11},{12,13},{... | collective-permute-start | bytes 9224 | tf_op jit(solution)/shard_map/ppermute | solution.py:25
  219.2 0.9 fusion.217
  220.1 5.5 %reshape.62 = f32[2,2,16,2,64,2]{5,4,3,2,1,0:T(8,128)} reshape(f32[4,32,128]{2,1,0:T(8,128)S(1)} %fusion.217) | data formatting | bytes 131072 | tf_op jit(solution)/shard_map/reshape | solution.py:79
  225.7 2.5 reduce_sum.88
  228.3 1.3 collective-permute-start.32
  229.6 5.2 %collective-permute-start.33 = (f32[1,16,64]{2,1,0:T(8,128)S(1)}, f32[1,16,64]{2,1,0:T(8,128)S(1)}, u32[]{:S(2)}, u32[]{:S(2)}) collective-permute-start(f32[1,16,64]{2,1,0:T(8,128)S(1)} %get-tuple-element.55), channel_id=1, source_target_pairs={{0,4},{4,8},{8,12},{12,16},{16,20},{20,24},{24,28},{1,5},{5,9},{9,... | collective-permute-start | bytes 12296 | tf_op jit(solution)/shard_map/ppermute | solution.py:25
  234.8 1.3 collective-permute-done.33
  236.2 1.3 collective-permute-start.34
  237.5 3.3 collective-permute-start.35
  241.8 1.3 collective-permute-start.36
  243.1 5.2 %collective-permute-start.37 = (f32[1,16,64]{2,1,0:T(8,128)S(1)}, f32[1,16,64]{2,1,0:T(8,128)S(1)}, u32[]{:S(2)}, u32[]{:S(2)}) collective-permute-start(f32[1,16,64]{2,1,0:T(8,128)S(1)} %get-tuple-element.53), channel_id=1, source_target_pairs={{0,4},{4,8},{8,12},{12,16},{16,20},{20,24},{24,28},{1,5},{5,9},{9,... | collective-permute-start | bytes 12296 | tf_op jit(solution)/shard_map/ppermute | solution.py:25
  248.4 1.3 collective-permute-done.37
  249.7 1.3 collective-permute-start.38
  250.9 5.0 %collective-permute-start.39 = (f32[4,1,64]{2,1,0:T(1,128)S(1)}, f32[4,1,64]{2,1,0:T(1,128)S(1)}, u32[]{:S(2)}, u32[]{:S(2)}) collective-permute-start(f32[4,1,64]{2,1,0:T(1,128)S(1)} %get-tuple-element.46), channel_id=1, source_target_pairs={{0,1},{1,2},{2,3},{4,5},{5,6},{6,7},{8,9},{9,10},{10,11},{12,13},{... | collective-permute-start | bytes 3080 | tf_op jit(solution)/shard_map/ppermute | solution.py:25
  256.0 47.5 %all-gather.1 = f32[32,1,256]{2,1,0:T(1,128)S(1)} all-gather(f32[1,1,256]{2,1,0:T(1,128)S(1)} %reshape.65), channel_id=1, replica_groups=mesh['xb'=8,'yb'=4] {'xb','yb'}, dimensions={0}, use_global_device_ids=true | all-gather | bytes 33792 | tf_op jit(solution)/shard_map/all_gather | solution.py:113
  304.3 36.6 %all-gather = f32[32,1,256]{2,1,0:T(1,128)S(1)} all-gather(f32[1,1,256]{2,1,0:T(1,128)S(1)} %reshape.63), channel_id=1, replica_groups=mesh['xb'=8,'yb'=4] {'xb','yb'}, dimensions={0}, use_global_device_ids=true | all-gather | bytes 33792 | tf_op jit(solution)/shard_map/all_gather | solution.py:112
  342.7 0.8 fusion.214
  (137 shorter events, 10.3 us)
Async XLA Ops:
  1.5 61.5 %collective-permute-start.1 = (f32[1,64,256]{2,1,0:T(8,128)S(1)}, f32[1,64,256]{2,1,0:T(8,128)S(1)}, u32[]{:S(2)}, u32[]{:S(2)}) collective-permute-start(f32[1,64,256]{2,1,0:T(8,128)S(1)} %get-tuple-element.31), channel_id=1, source_target_pairs={{0,4},{4,8},{8,12},{12,16},{16,20},{20,24},{24,28},{1,5},{5,9},{9,... | collective-permute-start | bytes 196616 | tf_op jit(solution)/shard_map/ppermute | solution.py:25
  6.4 56.7 %collective-permute-start = (f32[1,64,256]{2,1,0:T(8,128)S(1)}, f32[1,64,256]{2,1,0:T(8,128)S(1)}, u32[]{:S(2)}, u32[]{:S(2)}) collective-permute-start(f32[1,64,256]{2,1,0:T(8,128)S(1)} %get-tuple-element.30), channel_id=1, source_target_pairs={{4,0},{8,4},{12,8},{16,12},{20,16},{24,20},{28,24},{5,1},{9,5},{13... | collective-permute-start | bytes 196616 | tf_op jit(solution)/shard_map/ppermute | solution.py:28
  8.6 59.0 %collective-permute-start.5 = (f32[1,64,256]{2,1,0:T(8,128)S(1)}, f32[1,64,256]{2,1,0:T(8,128)S(1)}, u32[]{:S(2)}, u32[]{:S(2)}) collective-permute-start(f32[1,64,256]{2,1,0:T(8,128)S(1)} %get-tuple-element.33), channel_id=1, source_target_pairs={{0,4},{4,8},{8,12},{12,16},{16,20},{20,24},{24,28},{1,5},{5,9},{9,... | collective-permute-start | bytes 196616 | tf_op jit(solution)/shard_map/ppermute | solution.py:25
  13.1 54.5 %collective-permute-start.4 = (f32[1,64,256]{2,1,0:T(8,128)S(1)}, f32[1,64,256]{2,1,0:T(8,128)S(1)}, u32[]{:S(2)}, u32[]{:S(2)}) collective-permute-start(f32[1,64,256]{2,1,0:T(8,128)S(1)} %get-tuple-element.32), channel_id=1, source_target_pairs={{4,0},{8,4},{12,8},{16,12},{20,16},{24,20},{28,24},{5,1},{9,5},{13... | collective-permute-start | bytes 196616 | tf_op jit(solution)/shard_map/ppermute | solution.py:28
  50.1 12.9 %copy-start = (f32[8,64,256]{2,1,0:T(8,128)S(1)}, f32[8,64,256]{2,1,0:T(8,128)}, u32[]{:S(2)}) copy-start(f32[8,64,256]{2,1,0:T(8,128)} %param.5) | copy-start | bytes 1572868
  63.0 4.6 %copy-start.4 = (f32[8,64,256]{2,1,0:T(8,128)S(1)}, f32[8,64,256]{2,1,0:T(8,128)}, u32[]{:S(2)}) copy-start(f32[8,64,256]{2,1,0:T(8,128)} %param.3) | copy-start | bytes 1572868
  63.1 9.6 %collective-permute-start.2 = (f32[10,1,256]{2,1,0:T(1,128)S(1)}, f32[10,1,256]{2,1,0:T(1,128)S(1)}, u32[]{:S(2)}, u32[]{:S(2)}) collective-permute-start(f32[10,1,256]{2,1,0:T(1,128)S(1)} %get-tuple-element.23), channel_id=1, source_target_pairs={{1,0},{2,1},{3,2},{5,4},{6,5},{7,6},{9,8},{10,9},{11,10},{13,12},{... | collective-permute-start | bytes 30728 | tf_op jit(solution)/shard_map/ppermute | solution.py:28
  64.5 8.2 %collective-permute-start.3 = (f32[10,1,256]{2,1,0:T(1,128)S(1)}, f32[10,1,256]{2,1,0:T(1,128)S(1)}, u32[]{:S(2)}, u32[]{:S(2)}) collective-permute-start(f32[10,1,256]{2,1,0:T(1,128)S(1)} %get-tuple-element.22), channel_id=1, source_target_pairs={{0,1},{1,2},{2,3},{4,5},{5,6},{6,7},{8,9},{9,10},{10,11},{12,13},{... | collective-permute-start | bytes 30728 | tf_op jit(solution)/shard_map/ppermute | solution.py:25
  67.7 5.0 %copy-start.12 = (f32[1,64,256]{2,1,0:T(8,128)}, f32[1,64,256]{2,1,0:T(8,128)S(1)}, u32[]{:S(2)}) copy-start(f32[1,64,256]{2,1,0:T(8,128)S(1)} %collective-permute-done.4) | copy-start | bytes 196612
  67.7 5.5 %collective-permute-start.6 = (f32[10,1,256]{2,1,0:T(1,128)S(1)}, f32[10,1,256]{2,1,0:T(1,128)S(1)}, u32[]{:S(2)}, u32[]{:S(2)}) collective-permute-start(f32[10,1,256]{2,1,0:T(1,128)S(1)} %get-tuple-element.25), channel_id=1, source_target_pairs={{1,0},{2,1},{3,2},{5,4},{6,5},{7,6},{9,8},{10,9},{11,10},{13,12},{... | collective-permute-start | bytes 30728 | tf_op jit(solution)/shard_map/ppermute | solution.py:28
  69.0 4.5 %collective-permute-start.7 = (f32[10,1,256]{2,1,0:T(1,128)S(1)}, f32[10,1,256]{2,1,0:T(1,128)S(1)}, u32[]{:S(2)}, u32[]{:S(2)}) collective-permute-start(f32[10,1,256]{2,1,0:T(1,128)S(1)} %get-tuple-element.24), channel_id=1, source_target_pairs={{0,1},{1,2},{2,3},{4,5},{5,6},{6,7},{8,9},{9,10},{10,11},{12,13},{... | collective-permute-start | bytes 30728 | tf_op jit(solution)/shard_map/ppermute | solution.py:25
  72.7 1.3 copy-start.14
  72.7 1.2 copy-start.16
  73.2 1.0 copy-start.2
  73.2 1.0 copy-start.13
  74.2 8.9 %copy-start.11 = (f32[4,32,128]{2,1,0:T(8,128)S(1)}, f32[4,32,128]{2,1,0:T(8,128)}, u32[]{:S(2)}) copy-start(f32[4,32,128]{2,1,0:T(8,128)} %reduce_sum.87) | copy-start | bytes 196612
  76.2 7.2 %collective-permute-start.8 = (f32[1,64,256]{2,1,0:T(8,128)S(1)}, f32[1,64,256]{2,1,0:T(8,128)S(1)}, u32[]{:S(2)}, u32[]{:S(2)}) collective-permute-start(f32[1,64,256]{2,1,0:T(8,128)S(1)} %get-tuple-element.29), channel_id=1, source_target_pairs={{4,0},{8,4},{12,8},{16,12},{20,16},{24,20},{28,24},{5,1},{9,5},{13... | collective-permute-start | bytes 196616 | tf_op jit(solution)/shard_map/ppermute | solution.py:28
  77.5 8.6 %collective-permute-start.9 = (f32[1,64,256]{2,1,0:T(8,128)S(1)}, f32[1,64,256]{2,1,0:T(8,128)S(1)}, u32[]{:S(2)}, u32[]{:S(2)}) collective-permute-start(f32[1,64,256]{2,1,0:T(8,128)S(1)} %get-tuple-element.28), channel_id=1, source_target_pairs={{0,4},{4,8},{8,12},{12,16},{16,20},{20,24},{24,28},{1,5},{5,9},{9,... | collective-permute-start | bytes 196616 | tf_op jit(solution)/shard_map/ppermute | solution.py:25
  83.4 22.8 %copy-start.8 = (f32[1,64,256]{2,1,0:T(8,128)}, f32[1,64,256]{2,1,0:T(8,128)S(1)}, u32[]{:S(2)}) copy-start(f32[1,64,256]{2,1,0:T(8,128)S(1)} %collective-permute-done.8) | copy-start | bytes 196612
  86.2 20.0 %copy-start.9 = (f32[1,64,256]{2,1,0:T(8,128)}, f32[1,64,256]{2,1,0:T(8,128)S(1)}, u32[]{:S(2)}) copy-start(f32[1,64,256]{2,1,0:T(8,128)S(1)} %collective-permute-done.9) | copy-start | bytes 196612
  86.2 20.0 %collective-permute-start.10 = (f32[10,1,256]{2,1,0:T(1,128)S(1)}, f32[10,1,256]{2,1,0:T(1,128)S(1)}, u32[]{:S(2)}, u32[]{:S(2)}) collective-permute-start(f32[10,1,256]{2,1,0:T(1,128)S(1)} %get-tuple-element.21), channel_id=1, source_target_pairs={{1,0},{2,1},{3,2},{5,4},{6,5},{7,6},{9,8},{10,9},{11,10},{13,12},{... | collective-permute-start | bytes 30728 | tf_op jit(solution)/shard_map/ppermute | solution.py:28
  87.5 18.7 %collective-permute-start.11 = (f32[10,1,256]{2,1,0:T(1,128)S(1)}, f32[10,1,256]{2,1,0:T(1,128)S(1)}, u32[]{:S(2)}, u32[]{:S(2)}) collective-permute-start(f32[10,1,256]{2,1,0:T(1,128)S(1)} %get-tuple-element.20), channel_id=1, source_target_pairs={{0,1},{1,2},{2,3},{4,5},{5,6},{6,7},{8,9},{9,10},{10,11},{12,13},{... | collective-permute-start | bytes 30728 | tf_op jit(solution)/shard_map/ppermute | solution.py:25
  91.2 24.6 %collective-permute-start.16 = (f32[1,32,128]{2,1,0:T(8,128)}, f32[1,32,128]{2,1,0:T(8,128)}, u32[]{:S(2)}, u32[]{:S(2)}) collective-permute-start(f32[1,32,128]{2,1,0:T(8,128)} %get-tuple-element.45), channel_id=1, source_target_pairs={{4,0},{8,4},{12,8},{16,12},{20,16},{24,20},{28,24},{5,1},{9,5},{13... | collective-permute-start | bytes 49160 | tf_op jit(solution)/shard_map/ppermute | solution.py:28
  92.4 23.3 %collective-permute-start.17 = (f32[1,32,128]{2,1,0:T(8,128)}, f32[1,32,128]{2,1,0:T(8,128)}, u32[]{:S(2)}, u32[]{:S(2)}) collective-permute-start(f32[1,32,128]{2,1,0:T(8,128)} %get-tuple-element.44), channel_id=1, source_target_pairs={{0,4},{4,8},{8,12},{12,16},{16,20},{20,24},{24,28},{1,5},{5,9},{9,... | collective-permute-start | bytes 49160 | tf_op jit(solution)/shard_map/ppermute | solution.py:25
  106.1 1.1 copy-start.3
  106.2 1.2 copy-start.5
  106.2 1.2 copy-start.15
  106.2 1.2 copy-start.17
  106.2 0.6 copy-start.18
  106.2 0.6 copy-start.19
  109.5 21.0 %copy-start.1 = (f32[8,64,256]{2,1,0:T(8,128)}, f32[8,64,256]{2,1,0:T(8,128)S(1)}, u32[]{:S(2)}) copy-start(f32[8,64,256]{2,1,0:T(8,128)S(1)} %fusion.17) | copy-start | bytes 1572868
  109.5 13.1 %collective-permute-start.12 = (f32[1,64,256]{2,1,0:T(8,128)S(1)}, f32[1,64,256]{2,1,0:T(8,128)S(1)}, u32[]{:S(2)}, u32[]{:S(2)}) collective-permute-start(f32[1,64,256]{2,1,0:T(8,128)S(1)} %get-tuple-element.27), channel_id=1, source_target_pairs={{4,0},{8,4},{12,8},{16,12},{20,16},{24,20},{28,24},{5,1},{9,5},{13... | collective-permute-start | bytes 196616 | tf_op jit(solution)/shard_map/ppermute | solution.py:28
  110.8 11.8 %collective-permute-start.13 = (f32[1,64,256]{2,1,0:T(8,128)S(1)}, f32[1,64,256]{2,1,0:T(8,128)S(1)}, u32[]{:S(2)}, u32[]{:S(2)}) collective-permute-start(f32[1,64,256]{2,1,0:T(8,128)S(1)} %get-tuple-element.26), channel_id=1, source_target_pairs={{0,4},{4,8},{8,12},{12,16},{16,20},{20,24},{24,28},{1,5},{5,9},{9,... | collective-permute-start | bytes 196616 | tf_op jit(solution)/shard_map/ppermute | solution.py:25
  116.4 12.0 %collective-permute-start.18 = (f32[6,1,128]{2,1,0:T(1,128)S(1)}, f32[6,1,128]{2,1,0:T(1,128)S(1)}, u32[]{:S(2)}, u32[]{:S(2)}) collective-permute-start(f32[6,1,128]{2,1,0:T(1,128)S(1)} %get-tuple-element.39), channel_id=1, source_target_pairs={{1,0},{2,1},{3,2},{5,4},{6,5},{7,6},{9,8},{10,9},{11,10},{13,12},{... | collective-permute-start | bytes 9224 | tf_op jit(solution)/shard_map/ppermute | solution.py:28
  117.7 10.7 %collective-permute-start.19 = (f32[6,1,128]{2,1,0:T(1,128)S(1)}, f32[6,1,128]{2,1,0:T(1,128)S(1)}, u32[]{:S(2)}, u32[]{:S(2)}) collective-permute-start(f32[6,1,128]{2,1,0:T(1,128)S(1)} %get-tuple-element.38), channel_id=1, source_target_pairs={{0,1},{1,2},{2,3},{4,5},{5,6},{6,7},{8,9},{9,10},{10,11},{12,13},{... | collective-permute-start | bytes 9224 | tf_op jit(solution)/shard_map/ppermute | solution.py:25
  122.6 7.4 %collective-permute-start.14 = (f32[10,1,256]{2,1,0:T(1,128)S(1)}, f32[10,1,256]{2,1,0:T(1,128)S(1)}, u32[]{:S(2)}, u32[]{:S(2)}) collective-permute-start(f32[10,1,256]{2,1,0:T(1,128)S(1)} %get-tuple-element.19), channel_id=1, source_target_pairs={{1,0},{2,1},{3,2},{5,4},{6,5},{7,6},{9,8},{10,9},{11,10},{13,12},{... | collective-permute-start | bytes 30728 | tf_op jit(solution)/shard_map/ppermute | solution.py:28
  123.9 6.1 %collective-permute-start.15 = (f32[10,1,256]{2,1,0:T(1,128)S(1)}, f32[10,1,256]{2,1,0:T(1,128)S(1)}, u32[]{:S(2)}, u32[]{:S(2)}) collective-permute-start(f32[10,1,256]{2,1,0:T(1,128)S(1)} %get-tuple-element.18), channel_id=1, source_target_pairs={{0,1},{1,2},{2,3},{4,5},{5,6},{6,7},{8,9},{9,10},{10,11},{12,13},{... | collective-permute-start | bytes 30728 | tf_op jit(solution)/shard_map/ppermute | solution.py:25
  166.5 12.3 %copy-start.6 = (f32[6,34,130]{2,1,0:T(8,128)S(1)}, f32[6,34,130]{2,1,0:T(8,128)}, u32[]{:S(2)}) copy-start(f32[6,34,130]{2,1,0:T(8,128)} %select_maximum_fusion.20) | copy-start | bytes 318244
  179.7 6.5 %collective-permute-start.20 = (f32[1,32,128]{2,1,0:T(8,128)S(1)}, f32[1,32,128]{2,1,0:T(8,128)S(1)}, u32[]{:S(2)}, u32[]{:S(2)}) collective-permute-start(f32[1,32,128]{2,1,0:T(8,128)S(1)} %get-tuple-element.43), channel_id=1, source_target_pairs={{4,0},{8,4},{12,8},{16,12},{20,16},{24,20},{28,24},{5,1},{9,5},{13... | collective-permute-start | bytes 49160 | tf_op jit(solution)/shard_map/ppermute | solution.py:28
  181.0 6.6 %collective-permute-start.21 = (f32[1,32,128]{2,1,0:T(8,128)S(1)}, f32[1,32,128]{2,1,0:T(8,128)S(1)}, u32[]{:S(2)}, u32[]{:S(2)}) collective-permute-start(f32[1,32,128]{2,1,0:T(8,128)S(1)} %get-tuple-element.42), channel_id=1, source_target_pairs={{0,4},{4,8},{8,12},{12,16},{16,20},{20,24},{24,28},{1,5},{5,9},{9,... | collective-permute-start | bytes 49160 | tf_op jit(solution)/shard_map/ppermute | solution.py:25
  187.6 11.2 %collective-permute-start.22 = (f32[6,1,128]{2,1,0:T(1,128)S(1)}, f32[6,1,128]{2,1,0:T(1,128)S(1)}, u32[]{:S(2)}, u32[]{:S(2)}) collective-permute-start(f32[6,1,128]{2,1,0:T(1,128)S(1)} %get-tuple-element.37), channel_id=1, source_target_pairs={{1,0},{2,1},{3,2},{5,4},{6,5},{7,6},{9,8},{10,9},{11,10},{13,12},{... | collective-permute-start | bytes 9224 | tf_op jit(solution)/shard_map/ppermute | solution.py:28
  188.9 9.9 %collective-permute-start.23 = (f32[6,1,128]{2,1,0:T(1,128)S(1)}, f32[6,1,128]{2,1,0:T(1,128)S(1)}, u32[]{:S(2)}, u32[]{:S(2)}) collective-permute-start(f32[6,1,128]{2,1,0:T(1,128)S(1)} %get-tuple-element.36), channel_id=1, source_target_pairs={{0,1},{1,2},{2,3},{4,5},{5,6},{6,7},{8,9},{9,10},{10,11},{12,13},{... | collective-permute-start | bytes 9224 | tf_op jit(solution)/shard_map/ppermute | solution.py:25
  192.3 14.5 %collective-permute-start.28 = (f32[1,16,64]{2,1,0:T(8,128)S(1)}, f32[1,16,64]{2,1,0:T(8,128)S(1)}, u32[]{:S(2)}, u32[]{:S(2)}) collective-permute-start(f32[1,16,64]{2,1,0:T(8,128)S(1)} %get-tuple-element.58), channel_id=1, source_target_pairs={{4,0},{8,4},{12,8},{16,12},{20,16},{24,20},{28,24},{5,1},{9,5},{13... | collective-permute-start | bytes 12296 | tf_op jit(solution)/shard_map/ppermute | solution.py:28
  193.6 13.2 %collective-permute-start.29 = (f32[1,16,64]{2,1,0:T(8,128)S(1)}, f32[1,16,64]{2,1,0:T(8,128)S(1)}, u32[]{:S(2)}, u32[]{:S(2)}) collective-permute-start(f32[1,16,64]{2,1,0:T(8,128)S(1)} %get-tuple-element.57), channel_id=1, source_target_pairs={{0,4},{4,8},{8,12},{12,16},{16,20},{20,24},{24,28},{1,5},{5,9},{9,... | collective-permute-start | bytes 12296 | tf_op jit(solution)/shard_map/ppermute | solution.py:25
  199.9 25.8 %copy-start.7 = (f32[4,32,128]{2,1,0:T(8,128)}, f32[4,32,128]{2,1,0:T(8,128)S(1)}, u32[]{:S(2)}) copy-start(f32[4,32,128]{2,1,0:T(8,128)S(1)} %fusion.232) | copy-start | bytes 196612
  199.9 12.8 %collective-permute-start.24 = (f32[1,32,128]{2,1,0:T(8,128)S(1)}, f32[1,32,128]{2,1,0:T(8,128)S(1)}, u32[]{:S(2)}, u32[]{:S(2)}) collective-permute-start(f32[1,32,128]{2,1,0:T(8,128)S(1)} %get-tuple-element.41), channel_id=1, source_target_pairs={{4,0},{8,4},{12,8},{16,12},{20,16},{24,20},{28,24},{5,1},{9,5},{13... | collective-permute-start | bytes 49160 | tf_op jit(solution)/shard_map/ppermute | solution.py:28
  201.2 11.5 %collective-permute-start.25 = (f32[1,32,128]{2,1,0:T(8,128)S(1)}, f32[1,32,128]{2,1,0:T(8,128)S(1)}, u32[]{:S(2)}, u32[]{:S(2)}) collective-permute-start(f32[1,32,128]{2,1,0:T(8,128)S(1)} %get-tuple-element.40), channel_id=1, source_target_pairs={{0,4},{4,8},{8,12},{12,16},{16,20},{20,24},{24,28},{1,5},{5,9},{9,... | collective-permute-start | bytes 49160 | tf_op jit(solution)/shard_map/ppermute | solution.py:25
  206.9 11.4 %collective-permute-start.30 = (f32[4,1,64]{2,1,0:T(1,128)S(1)}, f32[4,1,64]{2,1,0:T(1,128)S(1)}, u32[]{:S(2)}, u32[]{:S(2)}) collective-permute-start(f32[4,1,64]{2,1,0:T(1,128)S(1)} %get-tuple-element.51), channel_id=1, source_target_pairs={{1,0},{2,1},{3,2},{5,4},{6,5},{7,6},{9,8},{10,9},{11,10},{13,12},{... | collective-permute-start | bytes 3080 | tf_op jit(solution)/shard_map/ppermute | solution.py:28
  208.2 10.1 %collective-permute-start.31 = (f32[4,1,64]{2,1,0:T(1,128)S(1)}, f32[4,1,64]{2,1,0:T(1,128)S(1)}, u32[]{:S(2)}, u32[]{:S(2)}) collective-permute-start(f32[4,1,64]{2,1,0:T(1,128)S(1)} %get-tuple-element.50), channel_id=1, source_target_pairs={{0,1},{1,2},{2,3},{4,5},{5,6},{6,7},{8,9},{9,10},{10,11},{12,13},{... | collective-permute-start | bytes 3080 | tf_op jit(solution)/shard_map/ppermute | solution.py:25
  212.7 5.7 %collective-permute-start.26 = (f32[6,1,128]{2,1,0:T(1,128)S(1)}, f32[6,1,128]{2,1,0:T(1,128)S(1)}, u32[]{:S(2)}, u32[]{:S(2)}) collective-permute-start(f32[6,1,128]{2,1,0:T(1,128)S(1)} %get-tuple-element.35), channel_id=1, source_target_pairs={{1,0},{2,1},{3,2},{5,4},{6,5},{7,6},{9,8},{10,9},{11,10},{13,12},{... | collective-permute-start | bytes 9224 | tf_op jit(solution)/shard_map/ppermute | solution.py:28
  214.0 5.1 %collective-permute-start.27 = (f32[6,1,128]{2,1,0:T(1,128)S(1)}, f32[6,1,128]{2,1,0:T(1,128)S(1)}, u32[]{:S(2)}, u32[]{:S(2)}) collective-permute-start(f32[6,1,128]{2,1,0:T(1,128)S(1)} %get-tuple-element.34), channel_id=1, source_target_pairs={{0,1},{1,2},{2,3},{4,5},{5,6},{6,7},{8,9},{9,10},{10,11},{12,13},{... | collective-permute-start | bytes 9224 | tf_op jit(solution)/shard_map/ppermute | solution.py:25
  228.3 6.5 %collective-permute-start.32 = (f32[1,16,64]{2,1,0:T(8,128)S(1)}, f32[1,16,64]{2,1,0:T(8,128)S(1)}, u32[]{:S(2)}, u32[]{:S(2)}) collective-permute-start(f32[1,16,64]{2,1,0:T(8,128)S(1)} %get-tuple-element.56), channel_id=1, source_target_pairs={{4,0},{8,4},{12,8},{16,12},{20,16},{24,20},{28,24},{5,1},{9,5},{13... | collective-permute-start | bytes 12296 | tf_op jit(solution)/shard_map/ppermute | solution.py:28
  229.6 6.5 %collective-permute-start.33 = (f32[1,16,64]{2,1,0:T(8,128)S(1)}, f32[1,16,64]{2,1,0:T(8,128)S(1)}, u32[]{:S(2)}, u32[]{:S(2)}) collective-permute-start(f32[1,16,64]{2,1,0:T(8,128)S(1)} %get-tuple-element.55), channel_id=1, source_target_pairs={{0,4},{4,8},{8,12},{12,16},{16,20},{20,24},{24,28},{1,5},{5,9},{9,... | collective-permute-start | bytes 12296 | tf_op jit(solution)/shard_map/ppermute | solution.py:25
  236.2 5.0 %collective-permute-start.34 = (f32[4,1,64]{2,1,0:T(1,128)S(1)}, f32[4,1,64]{2,1,0:T(1,128)S(1)}, u32[]{:S(2)}, u32[]{:S(2)}) collective-permute-start(f32[4,1,64]{2,1,0:T(1,128)S(1)} %get-tuple-element.49), channel_id=1, source_target_pairs={{1,0},{2,1},{3,2},{5,4},{6,5},{7,6},{9,8},{10,9},{11,10},{13,12},{... | collective-permute-start | bytes 3080 | tf_op jit(solution)/shard_map/ppermute | solution.py:28
  237.5 4.1 %collective-permute-start.35 = (f32[4,1,64]{2,1,0:T(1,128)S(1)}, f32[4,1,64]{2,1,0:T(1,128)S(1)}, u32[]{:S(2)}, u32[]{:S(2)}) collective-permute-start(f32[4,1,64]{2,1,0:T(1,128)S(1)} %get-tuple-element.48), channel_id=1, source_target_pairs={{0,1},{1,2},{2,3},{4,5},{5,6},{6,7},{8,9},{9,10},{10,11},{12,13},{... | collective-permute-start | bytes 3080 | tf_op jit(solution)/shard_map/ppermute | solution.py:25
  241.8 99.6 %copy-start.10 = (f32[2,16,64]{2,1,0:T(8,128)}, f32[2,16,64]{2,1,0:T(8,128)S(1)}, u32[]{:S(2)}) copy-start(f32[2,16,64]{2,1,0:T(8,128)S(1)} %fusion.270) | copy-start | bytes 24580
  241.8 6.6 %collective-permute-start.36 = (f32[1,16,64]{2,1,0:T(8,128)S(1)}, f32[1,16,64]{2,1,0:T(8,128)S(1)}, u32[]{:S(2)}, u32[]{:S(2)}) collective-permute-start(f32[1,16,64]{2,1,0:T(8,128)S(1)} %get-tuple-element.54), channel_id=1, source_target_pairs={{4,0},{8,4},{12,8},{16,12},{20,16},{24,20},{28,24},{5,1},{9,5},{13... | collective-permute-start | bytes 12296 | tf_op jit(solution)/shard_map/ppermute | solution.py:28
  243.1 6.5 %collective-permute-start.37 = (f32[1,16,64]{2,1,0:T(8,128)S(1)}, f32[1,16,64]{2,1,0:T(8,128)S(1)}, u32[]{:S(2)}, u32[]{:S(2)}) collective-permute-start(f32[1,16,64]{2,1,0:T(8,128)S(1)} %get-tuple-element.53), channel_id=1, source_target_pairs={{0,4},{4,8},{8,12},{12,16},{16,20},{20,24},{24,28},{1,5},{5,9},{9,... | collective-permute-start | bytes 12296 | tf_op jit(solution)/shard_map/ppermute | solution.py:25
  249.7 54.0 %collective-permute-start.38 = (f32[4,1,64]{2,1,0:T(1,128)S(1)}, f32[4,1,64]{2,1,0:T(1,128)S(1)}, u32[]{:S(2)}, u32[]{:S(2)}) collective-permute-start(f32[4,1,64]{2,1,0:T(1,128)S(1)} %get-tuple-element.47), channel_id=1, source_target_pairs={{1,0},{2,1},{3,2},{5,4},{6,5},{7,6},{9,8},{10,9},{11,10},{13,12},{... | collective-permute-start | bytes 3080 | tf_op jit(solution)/shard_map/ppermute | solution.py:28
  250.9 52.7 %collective-permute-start.39 = (f32[4,1,64]{2,1,0:T(1,128)S(1)}, f32[4,1,64]{2,1,0:T(1,128)S(1)}, u32[]{:S(2)}, u32[]{:S(2)}) collective-permute-start(f32[4,1,64]{2,1,0:T(1,128)S(1)} %get-tuple-element.46), channel_id=1, source_target_pairs={{0,1},{1,2},{2,3},{4,5},{5,6},{6,7},{8,9},{9,10},{10,11},{12,13},{... | collective-permute-start | bytes 3080 | tf_op jit(solution)/shard_map/ppermute | solution.py:25
where the time goes:
time: 347 us; the launch traced here: 345 us
  starting transfers between devices  117 us (34%)
  local copies, waits for them, and re-layouts  86 us (25%)
  blocking collectives  84.1 us (24%)
  other arithmetic  46.6 us (13%)
  waiting for transfers between devices  8.45 us (2%)
    ppermute x20, starting transfers between devices, with_halo(): lax.ppermute(lax.slice_in_dim(block, block.shape[dim] - width, None, axis...  91.3 us
    reshape x3, local copies, waits for them, and re-layouts, restrict_field(): field.reshape(sx // 2, 2, sy // 2, 2, sz // 2, 2).sum(axis=(1, 3, 5))  76.1 us
    all_gather x1, blocking collectives, collect_grid(): lax.all_gather(coefficient.reshape(1, -1), ('xb', 'yb'), axis=0, tiled=True)  47.5 us
    all_gather x1, blocking collectives, collect_grid(): lax.all_gather(right_side.reshape(1, -1), ('xb', 'yb'), axis=0, tiled=True)  36.6 us
    reduce_sum x7, other arithmetic, restrict_field(): field.reshape(sx // 2, 2, sy // 2, 2, sz // 2, 2).sum(axis=(1, 3, 5))  30.6 us
    ppermute x20, starting transfers between devices, with_halo(): lax.ppermute(lax.slice_in_dim(block, 0, width, axis=dim), axis, backward)  25.9 us
    ppermute x20, waiting for transfers between devices, with_halo(): lax.ppermute(lax.slice_in_dim(block, block.shape[dim] - width, None, axis...  8.12 us
  transfers between devices with their start and end apart: 40, of which 8 were waited for; matrix products, arithmetic and copies ran while one was open for 19% of the time, Pallas kernels for 0%

commit v1 on v0

v1 whole, which is shorter than its diff:
```python
import functools

import jax
import jax.numpy as jnp
from jax import lax
from jax.experimental import pallas as pl
from jax.experimental.pallas import tpu as pltpu
from jax.sharding import PartitionSpec as P

COARSE_ITERS = 8
MESH = pl.DeviceIdType.MESH

damping_alpha = 0.05
cheb_theta = 1.15
cheb_delta = 0.85
cheb_sigma = cheb_theta / cheb_delta
cheb_first = 1.0 / cheb_sigma
cheb_second = 1.0 / (2.0 * cheb_sigma - cheb_first)
cheb_carry = cheb_second * cheb_first
cheb_resid = 2.0 * cheb_second / cheb_delta
jacobi_weight = 0.8

K0, V0, E0, G0, K1, E1, G1, K2, E2 = range(9)


def lane_of(shape):
    return lax.broadcasted_iota(jnp.int32, shape, 1)


def row_of(shape):
    return lax.broadcasted_iota(jnp.int32, shape, 0)


def pair_matrix(rows, columns, valid, offset=0):
    source = row_of((rows, columns))
    target = lane_of((rows, columns)) - offset
    hit = (source // 2 == target) & (source < valid) & (target >= 0)
    return hit.astype(jnp.float32)


def fold_lanes(value, matrix):
    return jnp.dot(
        value, matrix, precision=lax.Precision.HIGHEST, preferred_element_type=jnp.float32
    )


def pair_rows(value, fold):
    n = value.shape[0]
    parts = []
    for t in range(value.shape[1] // 128):
        fold[t, 0:n, :] = value[:, 128 * t : 128 * (t + 1)]
        parts.append(
            fold[t, pl.ds(0, n // 2, stride=2), :] + fold[t, pl.ds(1, n // 2, stride=2), :]
        )
    return parts[0] if len(parts) == 1 else jnp.concatenate(parts, axis=1)


class Level:
    def __init__(self, dims, valid, scale, refs):
        self.nx, self.ny, self.lanes = dims
        self.valid = valid
        self.c = 0.5 * scale
        self.wx, self.wy, self.wl, self.wz, self.al, self.di = refs

    def inner_faces(self, k):
        shape = (self.ny, self.lanes)
        lane = lane_of(shape)
        for i in range(self.nx):
            own = k(i)
            if i + 1 < self.nx:
                self.wx[i + 1] = self.c * (own + k(i + 1))
            wz = self.c * (own + pltpu.roll(own, self.lanes - 1, 1))
            self.wz[i] = jnp.where(lane < self.valid - 1, wz, 0.0)
            edge = (lane == 0) | (lane == self.valid - 1)
            self.al[i] = damping_alpha + jnp.where(edge, self.c * own, 0.0)

    def y_faces(self, k, ky):
        shape = (self.ny, self.lanes)
        row = row_of(shape)
        for i in range(self.nx):
            own = k(i)
            up = jnp.where(row == self.ny - 1, ky[1, i : i + 1, :], pltpu.roll(own, self.ny - 1, 0))
            self.wy[i] = self.c * (own + up)
            self.wl[i : i + 1, :] = self.c * (own[0:1] + ky[0, i : i + 1, :])

    def x_faces(self, k, kx):
        self.wx[0] = self.c * (k(0) + kx[0])
        self.wx[self.nx] = self.c * (k(self.nx - 1) + kx[1])

    def diagonal(self, i):
        wz, wy = self.wz[i], self.wy[i]
        row = row_of((self.ny, self.lanes))
        below = jnp.where(row == 0, self.wl[i : i + 1, :], pltpu.roll(wy, 1, 0))
        total = self.al[i] + (wz + pltpu.roll(wz, 1, 1)) + (wy + below)
        self.di[i] = 1.0 / (total + (self.wx[i] + self.wx[i + 1]))

    def operate(self, i, v, vx, vy):
        shape = (self.ny, self.lanes)
        row = row_of(shape)
        own = v(i)
        fz = self.wz[i] * (own - pltpu.roll(own, self.lanes - 1, 1))
        result = self.al[i] * own + (fz - pltpu.roll(fz, 1, 1))
        over = vy[1, i : i + 1, :] if vy is not None else 0.0
        up = jnp.where(row == self.ny - 1, over, pltpu.roll(own, self.ny - 1, 0))
        fy = self.wy[i] * (own - up)
        low = self.wl[i : i + 1, :] * ((vy[0, i : i + 1, :] if vy is not None else 0.0) - own[0:1])
        result = result + (fy - jnp.where(row == 0, low, pltpu.roll(fy, 1, 0)))
        for face, j, side in ((i, i - 1, 0), (i + 1, i + 1, 1)):
            if 0 <= j < self.nx:
                result = result + self.wx[face] * (own - v(j))
            elif vx is not None:
                result = result + self.wx[face] * (own - vx[side])
            else:
                result = result + self.wx[face] * own
        return result


def kernel(nxb, nyb, v0_ref, f_ref, k_ref, fine, middle, lower, coarse, *scratch):
    names = []
    for l in range(3):
        fields = ("d0", "v1") if l == 0 else ("f%d" % l, "k%d" % l, "d%d" % l, "v2%d" % l)
        names += [*fields, *("%s%d" % (n, l) for n in ("wx", "wy", "wl", "wz", "al", "di", "fold"))]
    names += ["gx0", "gx1", "part", "kpart", "part_in", "kpart_in", "mine", "kmine"]
    names += ["whole", "kwhole", "last"]
    names += ["%s%d" % (n, e) for n in ("hx", "hy", "py") for e in range(9)]
    names += ["send", "recv", "psend", "precv", "kpsend", "kprecv"]
    names += ["wsend", "wrecv", "kwsend", "kwrecv"]
    s = dict(zip(names, scratch, strict=True))
    hx = [s["hx%d" % e] for e in range(9)]
    hy = [s["hy%d" % e] for e in range(9)]
    py = [s["py%d" % e] for e in range(9)]
    xi, yj = lax.axis_index("xb"), lax.axis_index("yb")
    has = (xi > 0, xi < nxb - 1, yj > 0, yj < nyb - 1)
    beside = (
        (jnp.maximum(xi - 1, 0), yj),
        (jnp.minimum(xi + 1, nxb - 1), yj),
        (xi, jnp.maximum(yj - 1, 0)),
        (xi, jnp.minimum(yj + 1, nyb - 1)),
    )

    barrier = pltpu.get_barrier_semaphore()

    def greet(device):
        pl.semaphore_signal(barrier, inc=1, device_id=device, device_id_type=MESH)

    for o in range(1, nyb):
        greet((xi, lax.rem(yj + o, nyb)))
    for side in (0, 1):
        @pl.when(has[side])
        def _():
            for y in range(nyb):
                greet((beside[side][0], jnp.int32(y)))
    for o in range(1, nxb):
        x = lax.rem(xi + o, nxb)

        @pl.when((x - xi > 1) | (xi - x > 1))
        def _():
            greet((x, yj))
    rows = has[0].astype(jnp.int32) + has[1].astype(jnp.int32)
    pl.semaphore_wait(barrier, (nyb - 1) + nyb * rows + (nxb - 1 - rows))

    def copy(e, side, src):
        dst = (hx if side < 2 else hy)[e].at[1 - side % 2]
        return pltpu.make_async_remote_copy(
            src_ref=src,
            dst_ref=dst,
            send_sem=s["send"].at[e, side],
            recv_sem=s["recv"].at[e, side],
            device_id=beside[side],
            device_id_type=MESH,
        )

    started = []

    def put(e, side, src):
        made = copy(e, side, src)
        pl.when(has[side])(made.start)
        started.append((made, side))
        away = (hx if side < 2 else hy)[e]

        @pl.when(jnp.logical_not(has[side]))
        def _():
            away[side % 2] = jnp.zeros(away.shape[1:], jnp.float32)

    def get(e, sides):
        for side in sides:
            other = side ^ 1
            buffer = (hx if side < 2 else hy)[e]
            made = pltpu.make_async_remote_copy(
                src_ref=buffer.at[side % 2],
                dst_ref=buffer.at[side % 2],
                send_sem=s["send"].at[e, other],
                recv_sem=s["recv"].at[e, other],
                device_id=beside[other],
                device_id_type=MESH,
            )
            pl.when(has[side])(made.wait_recv)

    def put_x(e, ref):
        put(e, 0, ref.at[0])
        put(e, 1, ref.at[ref.shape[0] - 1])

    def pack(e, i, value):
        n = value.shape[0]
        py[e][0, i : i + 1, :] = value[0:1]
        py[e][1, i : i + 1, :] = value[n - 1 : n]

    def put_y(e):
        put(e, 2, py[e].at[0])
        put(e, 3, py[e].at[1])

    def restrict(planes, matrix, fold, out):
        n = planes[0].shape[0]
        pairs = [planes[2 * i] + planes[2 * i + 1] for i in range(len(planes) // 2)]
        folded = fold_lanes(jnp.concatenate(pairs, axis=0), matrix) * 0.125
        summed = pair_rows(folded, fold)
        for i in range(len(pairs)):
            out[i] = summed[i * (n // 2) : (i + 1) * (n // 2)]

    def gather_rows(src, into, send, recv, offsets):
        made = []
        for t, step in enumerate(offsets):
            for o in range(nyb):
                if step == 0 and o == 0:
                    continue
                y = lax.rem(yj + o, nyb)
                side = 0 if step < 0 else 1
                x = xi if step == 0 else beside[side][0]
                one = pltpu.make_async_remote_copy(
                    src_ref=src.at[t],
                    dst_ref=into.at[t, yj],
                    send_sem=send.at[t, o],
                    recv_sem=recv.at[t, yj],
                    device_id=(x, y),
                    device_id_type=MESH,
                )
                if step == 0:
                    one.start()
                else:
                    pl.when(has[side])(one.start)
                made.append((one, step))
        return made

    def gathered_rows(src, into, send, recv, offsets):
        total = src[offsets.index(0)]
        for t, step in enumerate(offsets):
            for o in range(nyb):
                if step == 0 and o == 0:
                    continue
                y = lax.rem(yj + o, nyb)
                side = 1 if step < 0 else 0
                one = pltpu.make_async_remote_copy(
                    src_ref=into.at[t, y],
                    dst_ref=into.at[t, y],
                    send_sem=send.at[t, o],
                    recv_sem=recv.at[t, y],
                    device_id=(xi, lax.rem(yj + 1, nyb)),
                    device_id_type=MESH,
                )
                if step == 0:
                    one.wait_recv()
                else:
                    pl.when(has[side])(one.wait_recv)

                    @pl.when(jnp.logical_not(has[side]))
                    def _():
                        into[t, y] = jnp.zeros(into.shape[2:], jnp.float32)
                total = total + into[t, y]
        return total

    def gather_columns(src, into, send, recv):
        made = []
        for o in range(1, nxb):
            one = pltpu.make_async_remote_copy(
                src_ref=src,
                dst_ref=into.at[xi],
                send_sem=send.at[o],
                recv_sem=recv.at[xi],
                device_id=(lax.rem(xi + o, nxb), yj),
                device_id_type=MESH,
            )
            one.start()
            made.append(one)
        return made

    def gathered_columns(src, into, send, recv):
        into[xi] = src[...]
        for o in range(1, nxb):
            x = lax.rem(xi + o, nxb)
            pltpu.make_async_remote_copy(
                src_ref=into.at[x],
                dst_ref=into.at[x],
                send_sem=send.at[o],
                recv_sem=recv.at[x],
                device_id=(lax.rem(xi + 1, nxb), yj),
                device_id_type=MESH,
            ).wait_recv()

    nx, ny, nz = k_ref.shape
    levels = []
    for l in range(3):
        dims = (nx >> l, ny >> l, max(nz >> l, 128))
        refs = [s["%s%d" % (n, l)] for n in ("wx", "wy", "wl", "wz", "al", "di")]
        levels.append(Level(dims, nz >> l, 0.25**l, refs))
    low3, nz3 = ny // 8, nz // 8
    wide = nyb * nz3
    s01 = pair_matrix(nz, max(nz // 2, 128), nz)
    s12 = pair_matrix(max(nz // 2, 128), max(nz // 4, 128), nz // 2)

    def s23(offset):
        return pair_matrix(max(nz // 4, 128), wide, nz // 4, offset * nz3)

    put_x(K0, k_ref)
    put_x(V0, v0_ref)
    for i in range(nx):
        pack(K0, i, k_ref[i])
        pack(V0, i, v0_ref[i])
    put_y(K0)
    put_y(V0)

    restrict([k_ref[i] for i in range(nx)], s01, s["fold0"], s["k1"])
    put_x(K1, s["k1"])
    for i in range(nx // 2):
        pack(K1, i, s["k1"][i])
    put_y(K1)
    restrict([s["k1"][i] for i in range(nx // 2)], s12, s["fold1"], s["k2"])
    put_x(K2, s["k2"])
    for i in range(nx // 4):
        pack(K2, i, s["k2"][i])
    put_y(K2)
    restrict([s["k2"][i] for i in range(nx // 4)], s23(yj), s["fold2"], s["kpart"])
    kargs = (s["kpart"], s["kpart_in"], s["kpsend"], s["kprecv"], (0,))
    krows = gather_rows(*kargs)

    top = levels[0]
    inner, outer = list(range(1, nx - 1)), [0, nx - 1]
    k = lambda i: k_ref[i]
    v0 = lambda i: v0_ref[i]
    d0, v1 = s["d0"], s["v1"]
    top.inner_faces(k)
    get(K0, (2, 3))
    get(V0, (2, 3))
    top.y_faces(k, hy[K0])

    def first(i):
        top.diagonal(i)
        r = f_ref[i] - top.operate(i, v0, hx[V0], hy[V0])
        d = r * (top.di[i] * (1.0 / cheb_theta))
        d0[i] = d
        v = v0_ref[i] + d
        v1[i] = v
        pack(E0, i, v)

    for i in inner:
        first(i)
    get(K0, (0, 1))
    get(V0, (0, 1))
    top.x_faces(k, hx[K0])
    for i in outer:
        first(i)
    put_x(E0, v1)
    put_y(E0)

    s["kmine"][...] = gathered_rows(*kargs)
    kcargs = (s["kmine"], s["kwhole"], s["kwsend"], s["kwrecv"])
    kcolumns = gather_columns(*kcargs)
    for l, e, ref in ((1, K1, s["k1"]), (2, K2, s["k2"])):
        level = levels[l]
        kl = functools.partial(lambda ref, i: ref[i], ref)
        level.inner_faces(kl)
        get(e, (0, 1, 2, 3))
        level.y_faces(kl, hy[e])
        level.x_faces(kl, hx[e])
        for i in range(level.nx):
            level.diagonal(i)

    get(E0, (2, 3))

    def second(level, i, f, v1, d0, e, out):
        r = f(i) - level.operate(i, v1, hx[e], hy[e])
        v = v1(i) + (cheb_carry * d0(i) + (cheb_resid * level.di[i]) * r)
        out[i] = v
        return v

    f0 = lambda i: f_ref[i]
    v1at = lambda i: v1[i]
    d0at = lambda i: d0[i]
    for i in inner:
        second(top, i, f0, v1at, d0at, E0, fine)
    get(E0, (0, 1))
    for i in outer:
        second(top, i, f0, v1at, d0at, E0, fine)

    def face_sums(level, out, matrix, e, gx, fold):
        n = level.ny
        both = [level.wx[0] * out[0], level.wx[level.nx] * out[level.nx - 1]]
        folded = fold_lanes(jnp.concatenate(both, axis=0), matrix) * 0.125
        summed = pair_rows(folded, fold)
        for side in (0, 1):
            gx[side] = summed[side * (n // 2) : (side + 1) * (n // 2)]
        put_x(e, gx)
        lows, highs = [], []
        for i in range(level.nx // 2):
            a, b = 2 * i, 2 * i + 1
            lows.append(level.wl[a : a + 1, :] * out[a, 0:1, :] + level.wl[b : b + 1, :] * out[b, 0:1, :])
            highs.append(
                level.wy[a, n - 1 : n, :] * out[a, n - 1 : n, :]
                + level.wy[b, n - 1 : n, :] * out[b, n - 1 : n, :]
            )
        m = level.nx // 2
        pad = [jnp.zeros((8 - m, level.lanes), jnp.float32)]
        tops = [jnp.concatenate(part + pad, axis=0) for part in (lows, highs)]
        folded = fold_lanes(jnp.concatenate(tops, axis=0), matrix) * 0.125
        py[e][0] = folded[0:m]
        py[e][1] = folded[8 : 8 + m]
        put_y(e)

    def next_side(level, f, out, matrix, e, gx, fold, into):
        at = lambda i: out[i]
        face_sums(level, out, matrix, e, gx, fold)
        left = [f(i) - level.operate(i, at, None, None) for i in range(level.nx)]
        restrict(left, matrix, fold, into)
        get(e, (0, 1, 2, 3))
        m, n = level.nx // 2, level.ny // 2
        row = row_of((n, into.shape[2]))
        for i in range(m):
            value = into[i]
            if i == 0:
                value = value + hx[e][0]
            if i == m - 1:
                value = value + hx[e][1]
            value = value + jnp.where(row == 0, hy[e][0, i : i + 1, :], 0.0)
            into[i] = value + jnp.where(row == n - 1, hy[e][1, i : i + 1, :], 0.0)

    next_side(top, f0, fine, s01, G0, s["gx0"], s["fold0"], s["f1"])

    def correct(level, f, d, e, out):
        for i in range(level.nx):
            value = f[i] * (level.di[i] * (1.0 / cheb_theta))
            d[i] = value
            pack(e, i, value)
        put_x(e, d)
        put_y(e)
        get(e, (0, 1, 2, 3))
        at = lambda i: d[i]
        for i in range(level.nx):
            second(level, i, lambda i: f[i], at, at, e, out)

    correct(levels[1], s["f1"], s["d1"], E1, s["v21"])
    next_side(levels[1], lambda i: s["f1"][i], s["v21"], s12, G1, s["gx1"], s["fold1"], s["f2"])
    middle[...] = s["v21"][:, :, 0 : nz // 2]
    low = levels[2]
    correct(low, s["f2"], s["d2"], E2, s["v22"])

    v2, f2, part = s["v22"], s["f2"], s["part"]
    n = low.ny
    left = f2[0] - low.operate(0, lambda i: v2[i], None, None)
    left = left + (f2[1] - low.operate(1, lambda i: v2[i], None, None))
    stack = [left, low.wx[0] * v2[0], low.wx[2] * v2[1]]
    folded = fold_lanes(jnp.concatenate(stack, axis=0), s23(yj)) * 0.125
    summed = pair_rows(folded, s["fold2"])
    tiles = [summed[t * (n // 2) : (t + 1) * (n // 2)] for t in range(3)]
    down = low.wl[0:1, :] * v2[0, 0:1, :] + low.wl[1:2, :] * v2[1, 0:1, :]
    up = low.wy[0, n - 1 : n, :] * v2[0, n - 1 : n, :] + low.wy[1, n - 1 : n, :] * v2[1, n - 1 : n, :]
    eight = (8, low.lanes)
    down = fold_lanes(jnp.broadcast_to(down, eight), s23(yj - 1)) * 0.125
    up = fold_lanes(jnp.broadcast_to(up, eight), s23(yj + 1)) * 0.125
    row = row_of((low3, wide))
    own = tiles[0] + jnp.where(row == low3 - 1, down[0:1], 0.0) + jnp.where(row == 0, up[0:1], 0.0)
    part[0] = tiles[1]
    part[1] = own
    part[2] = tiles[2]
    fargs = (part, s["part_in"], s["psend"], s["precv"], (-1, 0, 1))
    frows = gather_rows(*fargs)
    lower[...] = v2[:, :, 0 : nz // 4]

    gathered_columns(*kcargs)
    shape = (nxb, wide)
    lane, xrow = lane_of(shape), row_of(shape)
    z = lax.rem(lane, nz3)
    inside = (xrow > 0, xrow < nxb - 1, z > 0, z < nz3 - 1)
    below = lane >= nz3
    above = lane < wide - nz3
    c = 0.5 * 0.25**3

    def around(v):
        first = jnp.where(below, pltpu.roll(v[-1], nz3, 1), 0.0)
        final = jnp.where(above, pltpu.roll(v[0], wide - nz3, 1), 0.0)
        out = []
        for r in range(low3):
            own = v[r]
            out.append(
                (
                    jnp.where(inside[0], pltpu.roll(own, 1, 0), 0.0),
                    jnp.where(inside[1], pltpu.roll(own, nxb - 1, 0), 0.0),
                    jnp.where(inside[2], pltpu.roll(own, 1, 1), 0.0),
                    jnp.where(inside[3], pltpu.roll(own, wide - 1, 1), 0.0),
                    v[r - 1] if r > 0 else first,
                    v[r + 1] if r < low3 - 1 else final,
                )
            )
        return out

    kc = [s["kwhole"][:, r, :] for r in range(low3)]
    weights = [[c * (kc[r] + other) for other in near] for r, near in enumerate(around(kc))]
    diagonal = [damping_alpha + sum(w) for w in weights]
    step = [jacobi_weight / d for d in diagonal]

    def operate(v):
        return [
            diagonal[r] * v[r] - sum(w * other for w, other in zip(weights[r], near))
            for r, near in enumerate(around(v))
        ]

    image = sum(operate([jnp.ones(shape, jnp.float32)] * low3))
    s["mine"][...] = gathered_rows(*fargs)
    fcargs = (s["mine"], s["whole"], s["wsend"], s["wrecv"])
    fcolumns = gather_columns(*fcargs)
    image = jnp.sum(image)
    gathered_columns(*fcargs)
    fc = [s["whole"][:, r, :] for r in range(low3)]
    v = [step[r] * fc[r] for r in range(low3)]
    for _ in range(COARSE_ITERS - 1):
        image_v = operate(v)
        v = [v[r] + step[r] * (fc[r] - image_v[r]) for r in range(low3)]
    image_v = operate(v)
    shift = jnp.sum(sum(fc[r] - image_v[r] for r in range(low3))) / image
    for r in range(low3):
        s["last"][:, r, :] = v[r] + shift
    block = s["last"][xi]
    coarse[0] = pltpu.roll(block, lax.rem(wide - yj * nz3, wide), 1)[:, 0:nz3]

    for made, side in started:
        pl.when(has[side])(made.wait_send)
    for made, step_x in krows + frows:
        if step_x == 0:
            made.wait_send()
        else:
            pl.when(has[0 if step_x < 0 else 1])(made.wait_send)
    for made in kcolumns + fcolumns:
        made.wait_send()


def per_device(nxb, nyb, initial_guess, right_side, coefficient):
    nx, ny, nz = coefficient.shape
    vm = lambda *shape: pltpu.VMEM(shape, jnp.float32)
    dma = lambda *shape: pltpu.SemaphoreType.DMA(shape)
    dims = [(nx >> l, ny >> l, max(nz >> l, 128)) for l in range(3)]
    low3, nz3 = ny // 8, nz // 8
    wide = nyb * nz3
    scratch = []
    for l, (a, b, c) in enumerate(dims):
        if l == 0:
            scratch += [vm(a, b, c), vm(a, b, c)]
        else:
            scratch += [vm(a, b, c)] * 4
        scratch += [vm(a + 1, b, c), vm(a, b, c), vm(a, c), vm(a, b, c), vm(a, b, c), vm(a, b, c)]
        folded = dims[l + 1][2] if l < 2 else wide
        scratch += [vm(folded // 128, max(a // 2, 3) * b + 8, 128)]
    scratch += [vm(2, *dims[1][1:]), vm(2, *dims[2][1:])]
    scratch += [vm(3, low3, wide), vm(1, low3, wide), vm(3, nyb, low3, wide), vm(1, nyb, low3, wide)]
    scratch += [vm(low3, wide), vm(low3, wide)] + [vm(nxb, low3, wide)] * 3
    where = (0, 0, 0, 1, 1, 1, 2, 2, 2)
    scratch += [vm(2, *dims[l][1:]) for l in where]
    scratch += [vm(2, dims[l][0], dims[l][2]) for l in where] * 2
    scratch += [dma(9, 4), dma(9, 4), dma(3, nyb), dma(3, nyb), dma(1, nyb), dma(1, nyb)]
    scratch += [dma(nxb)] * 4
    block = lambda l: jax.ShapeDtypeStruct((nx >> l, ny >> l, nz >> l), jnp.float32)
    whole = pl.BlockSpec(memory_space=pltpu.VMEM)
    return pl.pallas_call(
        functools.partial(kernel, nxb, nyb),
        out_shape=[block(0), block(1), block(2), block(3)],
        in_specs=[whole] * 3,
        out_specs=[whole] * 4,
        scratch_shapes=scratch,
        compiler_params=pltpu.CompilerParams(
            collective_id=0, has_side_effects=True, vmem_limit_bytes=40 * 1024 * 1024
        ),
    )(initial_guess, right_side, coefficient)


def solution(mesh):
    placed = P("xb", "yb", None)
    return jax.shard_map(
        functools.partial(per_device, mesh.shape["xb"], mesh.shape["yb"]),
        mesh=mesh,
        in_specs=(placed,) * 3,
        out_specs=(placed,) * 4,
        check_vma=False,
    )
```

time: 347 us -> 48.4 us (0.14)
  starting transfers between devices: 117 us -> 0 us
  blocking collectives: 84.1 us -> 0 us
  local copies, waits for them, and re-layouts: 86 us -> 5.74 us
  other arithmetic: 46.6 us -> 0 us
  Pallas kernels: 0 us -> 41.7 us
  waiting for transfers between devices: 8.45 us -> 0 us
    ppermute x40 -> x0, starting transfers between devices: 117 us -> none  [the longest x20 91.3 us: with_halo(): lax.ppermute(lax.slice_in_dim(block, block.shape[dim] - width, None, axis...]
    all_gather x2 -> x0, blocking collectives: 84.1 us -> none  [the longest x1 47.5 us: collect_grid(): lax.all_gather(coefficient.reshape(1, -1), ('xb', 'yb'), axis=0, tiled=True)]
    reshape x3 -> x0, local copies, waits for them, and re-layouts: 76.1 us -> none  [restrict_field(): field.reshape(sx // 2, 2, sy // 2, 2, sz // 2, 2).sum(axis=(1, 3, 5))]
    pallas_call x0 -> x1, Pallas kernels: none -> 41.7 us  [per_device(): pl.pallas_call(functools.partial(kernel, nxb, nyb), out_shape=[block(0),...]
    reduce_sum x8 -> x0, other arithmetic: 31.4 us -> none  [the longest x7 30.6 us: restrict_field(): field.reshape(sx // 2, 2, sy // 2, 2, sz // 2, 2).sum(axis=(1, 3, 5))]
    ppermute x40 -> x0, waiting for transfers between devices: 8.45 us -> none  [the longest x20 8.12 us: with_halo(): lax.ppermute(lax.slice_in_dim(block, block.shape[dim] - width, None, axis...]
    add x12 -> x0, other arithmetic: 6.99 us -> none  [the longest x3 3.13 us: smooth_level(): second = first + second_step]
    mul x1 -> x0, local copies, waits for them, and re-layouts: 5.53 us -> none  [restrict_field(): field.reshape(sx // 2, 2, sy // 2, 2, sz // 2, 2).sum(axis=(1, 3, 5))]
  transfers between devices with their start and end apart: 40 -> 0, of which waited for: 8 -> 0; matrix products, arithmetic and copies ran while one was open for 19% -> 0% of each run, Pallas kernels for 0% -> 0%
where the time goes in v1:
time: 48.4 us; the launch traced here: 48.1 us
  Pallas kernels  41.7 us (86%)
  local copies, waits for them, and re-layouts  5.74 us (12%)
  between operations  0.65 us (1%)
    pallas_call x1, Pallas kernels, per_device(): pl.pallas_call(functools.partial(kernel, nxb, nyb), out_shape=[block(0),...  41.7 us
    unnamed x10, local copies, waits for them, and re-layouts  5.74 us

profile of v1, /device:TPU:0, one launch (start us, length us, event | category | flops | bytes accessed | tf_op | source)
XLA Modules:
  0.0 48.1 jit_solution(1489513862144493685)
XLA Ops:
  0.6 0.0 copy-start
  0.6 1.0 %copy-done = f32[8,64,256]{2,1,0:T(8,128)S(1)} copy-done((f32[8,64,256]{2,1,0:T(8,128)S(1)}, f32[8,64,256]{2,1,0:T(8,128)}, u32[]{:S(2)}) %copy-start) | copy-done | bytes 524312
  1.7 0.0 copy-start.1
  1.7 1.0 %copy-done.1 = f32[8,64,256]{2,1,0:T(8,128)S(1)} copy-done((f32[8,64,256]{2,1,0:T(8,128)S(1)}, f32[8,64,256]{2,1,0:T(8,128)}, u32[]{:S(2)}) %copy-start.1) | copy-done | bytes 524312
  2.7 0.0 copy-start.2
  2.7 1.0 %copy-done.2 = f32[8,64,256]{2,1,0:T(8,128)S(1)} copy-done((f32[8,64,256]{2,1,0:T(8,128)S(1)}, f32[8,64,256]{2,1,0:T(8,128)}, u32[]{:S(2)}) %copy-start.2) | copy-done | bytes 524312
  3.8 41.7 %shard_map.66 = (f32[8,64,256]{2,1,0:T(8,128)S(1)}, f32[4,32,128]{2,1,0:T(8,128)S(1)}, f32[2,16,64]{2,1,0:T(8,128)S(1)}, f32[1,8,32]{2,1,0:T(8,128)S(1)}) custom-call(f32[8,64,256]{2,1,0:T(8,128)S(1)} %copy-done, f32[8,64,256]{2,1,0:T(8,128)S(1)} %copy-done.1, f32[8,64,256]{2,1,0:T(8,128)S(1)} %copy-done.2), custom_call_target="tpu_custom_call" | custom-call | tf_op jit(solution)/shard_map/pallas_call | solution.py:570
  45.5 0.8 %copy.11 = f32[8,64,256]{2,1,0:T(8,128)} copy(f32[8,64,256]{2,1,0:T(8,128)S(1)} %get-tuple-element.8) | data formatting | bytes 1048576
  46.3 0.6 %copy.12 = f32[4,32,128]{2,1,0:T(8,128)} copy(f32[4,32,128]{2,1,0:T(8,128)S(1)} %get-tuple-element.9) | data formatting | bytes 131072
  46.9 0.6 %copy.13 = f32[2,16,64]{2,1,0:T(8,128)} copy(f32[2,16,64]{2,1,0:T(8,128)S(1)} %get-tuple-element.10) | data formatting | bytes 16384
  47.5 0.6 %copy.14 = f32[1,8,32]{2,1,0:T(8,128)} copy(f32[1,8,32]{2,1,0:T(8,128)S(1)} %get-tuple-element.11) | data formatting | bytes 2048
Async XLA Ops:
  0.6 1.0 %copy-start = (f32[8,64,256]{2,1,0:T(8,128)S(1)}, f32[8,64,256]{2,1,0:T(8,128)}, u32[]{:S(2)}) copy-start(f32[8,64,256]{2,1,0:T(8,128)} %v0_ref.1) | copy-start | bytes 1572868
  1.7 1.0 %copy-start.1 = (f32[8,64,256]{2,1,0:T(8,128)S(1)}, f32[8,64,256]{2,1,0:T(8,128)}, u32[]{:S(2)}) copy-start(f32[8,64,256]{2,1,0:T(8,128)} %f_ref.1) | copy-start | bytes 1572868
  2.7 1.0 %copy-start.2 = (f32[8,64,256]{2,1,0:T(8,128)S(1)}, f32[8,64,256]{2,1,0:T(8,128)}, u32[]{:S(2)}) copy-start(f32[8,64,256]{2,1,0:T(8,128)} %k_ref.1) | copy-start | bytes 1572868

commit v2 on v1

--- a/solution.py
+++ b/solution.py
@@ -35,13 +35,23 @@
     source = row_of((rows, columns))
     target = lane_of((rows, columns)) - offset
     hit = (source // 2 == target) & (source < valid) & (target >= 0)
-    return hit.astype(jnp.float32)
+    return jnp.where(hit, 1.0, 0.0).astype(jnp.bfloat16)
 
 
 def fold_lanes(value, matrix):
-    return jnp.dot(
-        value, matrix, precision=lax.Precision.HIGHEST, preferred_element_type=jnp.float32
-    )
+    n = value.shape[0]
+    high = value.astype(jnp.bfloat16)
+    rest = value - high.astype(jnp.float32)
+    middle = rest.astype(jnp.bfloat16)
+    lowest = (rest - middle.astype(jnp.float32)).astype(jnp.bfloat16)
+    if n % 16 == 0:
+        parts = jnp.concatenate([high, middle, lowest], axis=0)
+        out = jnp.dot(parts, matrix, preferred_element_type=jnp.float32)
+        return out[0:n] + (out[n : 2 * n] + out[2 * n : 3 * n])
+    out = [
+        jnp.dot(p, matrix, preferred_element_type=jnp.float32) for p in (high, middle, lowest)
+    ]
+    return out[0] + (out[1] + out[2])
 
 
 def pair_rows(value, fold):
@@ -115,7 +125,7 @@
         return result
 
 
-def kernel(nxb, nyb, v0_ref, f_ref, k_ref, fine, middle, lower, coarse, *scratch):
+def kernel(nxb, nyb, v0_hbm, f_hbm, k_hbm, *rest):
     names = []
     for l in range(3):
         fields = ("d0", "v1") if l == 0 else ("f%d" % l, "k%d" % l, "d%d" % l, "v2%d" % l)
@@ -124,8 +134,12 @@
     names += ["whole", "kwhole", "last"]
     names += ["%s%d" % (n, e) for n in ("hx", "hy", "py") for e in range(9)]
     names += ["send", "recv", "psend", "precv", "kpsend", "kprecv"]
-    names += ["wsend", "wrecv", "kwsend", "kwrecv"]
-    s = dict(zip(names, scratch, strict=True))
+    names += ["wsend", "wrecv", "kwsend", "kwrecv", "v0", "f0", "k0", "load"]
+    names += ["fine", "middle", "lower", "coarse", "store"]
+    s = dict(zip(names, rest[4:], strict=True))
+    held = [s[n] for n in ("fine", "middle", "lower", "coarse")]
+    fine, middle, lower, coarse = held
+    stores = [pltpu.make_async_copy(held[t], rest[t], s["store"].at[t]) for t in range(4)]
     hx = [s["hx%d" % e] for e in range(9)]
     hy = [s["hy%d" % e] for e in range(9)]
     py = [s["py%d" % e] for e in range(9)]
@@ -137,6 +151,14 @@
         (xi, jnp.maximum(yj - 1, 0)),
         (xi, jnp.minimum(yj + 1, nyb - 1)),
     )
+
+    v0_ref, f_ref, k_ref = s["v0"], s["f0"], s["k0"]
+    loads = [
+        pltpu.make_async_copy(source, target, s["load"].at[t])
+        for t, (source, target) in enumerate(((k_hbm, k_ref), (v0_hbm, v0_ref), (f_hbm, f_ref)))
+    ]
+    for one in loads:
+        one.start()
 
     barrier = pltpu.get_barrier_semaphore()
 
@@ -209,13 +231,13 @@
         put(e, 2, py[e].at[0])
         put(e, 3, py[e].at[1])
 
-    def restrict(planes, matrix, fold, out):
+    def restrict(planes, matrix, fold, out, start=0):
         n = planes[0].shape[0]
         pairs = [planes[2 * i] + planes[2 * i + 1] for i in range(len(planes) // 2)]
         folded = fold_lanes(jnp.concatenate(pairs, axis=0), matrix) * 0.125
         summed = pair_rows(folded, fold)
         for i in range(len(pairs)):
-            out[i] = summed[i * (n // 2) : (i + 1) * (n // 2)]
+            out[start + i] = summed[i * (n // 2) : (i + 1) * (n // 2)]
 
     def gather_rows(src, into, send, recv, offsets):
         made = []
@@ -310,12 +332,15 @@
     def s23(offset):
         return pair_matrix(max(nz // 4, 128), wide, nz // 4, offset * nz3)
 
-    put_x(K0, k_ref)
-    put_x(V0, v0_ref)
+    put_x(K0, k_hbm)
+    put_x(V0, v0_hbm)
+    loads[0].wait()
     for i in range(nx):
         pack(K0, i, k_ref[i])
+    put_y(K0)
+    loads[1].wait()
+    for i in range(nx):
         pack(V0, i, v0_ref[i])
-    put_y(K0)
     put_y(V0)
 
     restrict([k_ref[i] for i in range(nx)], s01, s["fold0"], s["k1"])
@@ -338,6 +363,7 @@
     v0 = lambda i: v0_ref[i]
     d0, v1 = s["d0"], s["v1"]
     top.inner_faces(k)
+    loads[2].wait()
     get(K0, (2, 3))
     get(V0, (2, 3))
     top.y_faces(k, hy[K0])
@@ -358,7 +384,7 @@
     top.x_faces(k, hx[K0])
     for i in outer:
         first(i)
-    put_x(E0, v1)
+        put(E0, 0 if i == 0 else 1, v1.at[i])
     put_y(E0)
 
     s["kmine"][...] = gathered_rows(*kargs)
@@ -385,12 +411,6 @@
     f0 = lambda i: f_ref[i]
     v1at = lambda i: v1[i]
     d0at = lambda i: d0[i]
-    for i in inner:
-        second(top, i, f0, v1at, d0at, E0, fine)
-    get(E0, (0, 1))
-    for i in outer:
-        second(top, i, f0, v1at, d0at, E0, fine)
-
     def face_sums(level, out, matrix, e, gx, fold):
         n = level.ny
         both = [level.wx[0] * out[0], level.wx[level.nx] * out[level.nx - 1]]
@@ -415,11 +435,16 @@
         py[e][1] = folded[8 : 8 + m]
         put_y(e)
 
-    def next_side(level, f, out, matrix, e, gx, fold, into):
+    def left_over(level, f, out, pair, matrix, fold, into):
         at = lambda i: out[i]
+        left = [f(i) - level.operate(i, at, None, None) for i in (2 * pair, 2 * pair + 1)]
+        restrict(left, matrix, fold, into, pair)
+
+    def next_side(level, f, out, matrix, e, gx, fold, into, done=()):
         face_sums(level, out, matrix, e, gx, fold)
-        left = [f(i) - level.operate(i, at, None, None) for i in range(level.nx)]
-        restrict(left, matrix, fold, into)
+        for pair in range(level.nx // 2):
+            if pair not in done:
+                left_over(level, f, out, pair, matrix, fold, into)
         get(e, (0, 1, 2, 3))
         m, n = level.nx // 2, level.ny // 2
         row = row_of((n, into.shape[2]))
@@ -432,7 +457,17 @@
             value = value + jnp.where(row == 0, hy[e][0, i : i + 1, :], 0.0)
             into[i] = value + jnp.where(row == n - 1, hy[e][1, i : i + 1, :], 0.0)
 
-    next_side(top, f0, fine, s01, G0, s["gx0"], s["fold0"], s["f1"])
+    for i in inner:
+        second(top, i, f0, v1at, d0at, E0, fine)
+    middle_pairs = tuple(range(1, nx // 2 - 1))
+    for pair in middle_pairs:
+        left_over(top, f0, fine, pair, s01, s["fold0"], s["f1"])
+    get(E0, (0, 1))
+    for i in outer:
+        second(top, i, f0, v1at, d0at, E0, fine)
+
+    stores[0].start()
+    next_side(top, f0, fine, s01, G0, s["gx0"], s["fold0"], s["f1"], middle_pairs)
 
     def correct(level, f, d, e, out):
         for i in range(level.nx):
@@ -449,6 +484,7 @@
     correct(levels[1], s["f1"], s["d1"], E1, s["v21"])
     next_side(levels[1], lambda i: s["f1"][i], s["v21"], s12, G1, s["gx1"], s["fold1"], s["f2"])
     middle[...] = s["v21"][:, :, 0 : nz // 2]
+    stores[1].start()
     low = levels[2]
     correct(low, s["f2"], s["d2"], E2, s["v22"])
 
@@ -473,6 +509,7 @@
     fargs = (part, s["part_in"], s["psend"], s["precv"], (-1, 0, 1))
     frows = gather_rows(*fargs)
     lower[...] = v2[:, :, 0 : nz // 4]
+    stores[2].start()
 
     gathered_columns(*kcargs)
     shape = (nxb, wide)
@@ -529,7 +566,10 @@
         s["last"][:, r, :] = v[r] + shift
     block = s["last"][xi]
     coarse[0] = pltpu.roll(block, lax.rem(wide - yj * nz3, wide), 1)[:, 0:nz3]
-
+    stores[3].start()
+
+    for one in stores:
+        one.wait()
     for made, side in started:
         pl.when(has[side])(made.wait_send)
     for made, step_x in krows + frows:
@@ -539,6 +579,15 @@
             pl.when(has[0 if step_x < 0 else 1])(made.wait_send)
     for made in kcolumns + fcolumns:
         made.wait_send()
+
+
+def write_out(*refs):
+    sem = refs[8]
+    copies = [pltpu.make_async_copy(refs[t], refs[4 + t], sem.at[t]) for t in range(4)]
+    for one in copies:
+        one.start()
+    for one in copies:
+        one.wait()
 
 
 def per_device(nxb, nyb, initial_guess, right_side, coefficient):
@@ -565,18 +614,28 @@
     scratch += [vm(2, dims[l][0], dims[l][2]) for l in where] * 2
     scratch += [dma(9, 4), dma(9, 4), dma(3, nyb), dma(3, nyb), dma(1, nyb), dma(1, nyb)]
     scratch += [dma(nxb)] * 4
+    scratch += [vm(nx, ny, nz)] * 3 + [dma(3)]
+    scratch += [vm(nx >> l, ny >> l, nz >> l) for l in range(4)] + [dma(4)]
     block = lambda l: jax.ShapeDtypeStruct((nx >> l, ny >> l, nz >> l), jnp.float32)
-    whole = pl.BlockSpec(memory_space=pltpu.VMEM)
-    return pl.pallas_call(
+    anywhere = pl.BlockSpec(memory_space=pl.ANY)
+    fields = pl.pallas_call(
         functools.partial(kernel, nxb, nyb),
         out_shape=[block(0), block(1), block(2), block(3)],
-        in_specs=[whole] * 3,
-        out_specs=[whole] * 4,
+        in_specs=[anywhere] * 3,
+        out_specs=[anywhere] * 4,
         scratch_shapes=scratch,
         compiler_params=pltpu.CompilerParams(
-            collective_id=0, has_side_effects=True, vmem_limit_bytes=40 * 1024 * 1024
+            collective_id=0, has_side_effects=True, vmem_limit_bytes=56 * 1024 * 1024
         ),
     )(initial_guess, right_side, coefficient)
+    return pl.pallas_call(
+        write_out,
+        out_shape=[block(0), block(1), block(2), block(3)],
+        in_specs=[anywhere] * 4,
+        out_specs=[anywhere] * 4,
+        scratch_shapes=[dma(4)],
+        compiler_params=pltpu.CompilerParams(vmem_limit_bytes=56 * 1024 * 1024),
+    )(*fields)
 
 
 def solution(mesh):

time: 48.4 us -> 62.7 us (1.30)
  Pallas kernels: 41.7 us -> 61.9 us
  local copies, waits for them, and re-layouts: 5.74 us -> 0 us
    pallas_call x0 -> x1, Pallas kernels: none -> 19.6 us  [per_device(): pl.pallas_call(write_out, out_shape=[block(0), block(1), block(2), block(...]
    unnamed x10 -> x0, local copies, waits for them, and re-layouts: 5.74 us -> none
where the time goes in v2:
time: 62.7 us; the launch traced here: 62.6 us
  Pallas kernels  61.9 us (99%)
  between operations  0.64 us (1%)
    pallas_call x1, Pallas kernels, per_device(): pl.pallas_call(functools.partial(kernel, nxb, nyb), out_shape=[block(0),...  42.3 us
    pallas_call x1, Pallas kernels, per_device(): pl.pallas_call(write_out, out_shape=[block(0), block(1), block(2), block(...  19.6 us

profile of v2, /device:TPU:0, one launch (start us, length us, event | category | flops | bytes accessed | tf_op | source)
XLA Modules:
  0.0 62.6 jit_solution(1483167796795188731)
XLA Ops:
  0.6 42.3 %shard_map.66 = (f32[8,64,256]{2,1,0:T(8,128)}, f32[4,32,128]{2,1,0:T(8,128)}, f32[2,16,64]{2,1,0:T(8,128)}, f32[1,8,32]{2,1,0:T(8,128)}) custom-call(f32[8,64,256]{2,1,0:T(8,128)} %v0_hbm.1, f32[8,64,256]{2,1,0:T(8,128)} %f_hbm.1, f32[8,64,256]{2,1,0:T(8,128)} %k_hbm.1), custom_call_target="tpu_custom_call" | custom-call | tf_op jit(solution)/shard_map/pallas_call | solution.py:621
  42.9 19.6 %shard_map.67 = (f32[8,64,256]{2,1,0:T(8,128)}, f32[4,32,128]{2,1,0:T(8,128)}, f32[2,16,64]{2,1,0:T(8,128)}, f32[1,8,32]{2,1,0:T(8,128)}) custom-call(f32[8,64,256]{2,1,0:T(8,128)} %get-tuple-element.8.refs_0_, f32[4,32,128]{2,1,0:T(8,128)} %get-tuple-element.9.refs_1_, f32[2,16,64]{2,1,0:T(8,128)} %get-tuple-element.10.refs_2_, ...), custom_call_target="tpu_custom_call" | custom-call | tf_op jit(solution)/shard_map/pallas_call | solution.py:631

commit v3 on v2

--- a/solution.py
+++ b/solution.py
@@ -72,26 +72,43 @@
         self.c = 0.5 * scale
         self.wx, self.wy, self.wl, self.wz, self.al, self.di = refs
 
+    def planes(self, body):
+        if self.nx > 4:
+            pl.loop(0, self.nx)(body)
+        else:
+            for i in range(self.nx):
+                body(i)
+
     def inner_faces(self, k):
         shape = (self.ny, self.lanes)
         lane = lane_of(shape)
-        for i in range(self.nx):
+        for i in range(self.nx - 1) if self.nx <= 4 else ():
+            self.wx[i + 1] = self.c * (k(i) + k(i + 1))
+        if self.nx > 4:
+            @pl.loop(0, self.nx - 1)
+            def _(i):
+                self.wx[i + 1] = self.c * (k(i) + k(i + 1))
+
+        def body(i):
             own = k(i)
-            if i + 1 < self.nx:
-                self.wx[i + 1] = self.c * (own + k(i + 1))
             wz = self.c * (own + pltpu.roll(own, self.lanes - 1, 1))
             self.wz[i] = jnp.where(lane < self.valid - 1, wz, 0.0)
             edge = (lane == 0) | (lane == self.valid - 1)
             self.al[i] = damping_alpha + jnp.where(edge, self.c * own, 0.0)
 
+        self.planes(body)
+
     def y_faces(self, k, ky):
         shape = (self.ny, self.lanes)
         row = row_of(shape)
-        for i in range(self.nx):
+
+        def body(i):
             own = k(i)
-            up = jnp.where(row == self.ny - 1, ky[1, i : i + 1, :], pltpu.roll(own, self.ny - 1, 0))
+            up = jnp.where(row == self.ny - 1, ky[1, pl.ds(i, 1), :], pltpu.roll(own, self.ny - 1, 0))
             self.wy[i] = self.c * (own + up)
-            self.wl[i : i + 1, :] = self.c * (own[0:1] + ky[0, i : i + 1, :])
+            self.wl[pl.ds(i, 1), :] = self.c * (own[0:1] + ky[0, pl.ds(i, 1), :])
+
+        self.planes(body)
 
     def x_faces(self, k, kx):
         self.wx[0] = self.c * (k(0) + kx[0])
@@ -100,7 +117,7 @@
     def diagonal(self, i):
         wz, wy = self.wz[i], self.wy[i]
         row = row_of((self.ny, self.lanes))
-        below = jnp.where(row == 0, self.wl[i : i + 1, :], pltpu.roll(wy, 1, 0))
+        below = jnp.where(row == 0, self.wl[pl.ds(i, 1), :], pltpu.roll(wy, 1, 0))
         total = self.al[i] + (wz + pltpu.roll(wz, 1, 1)) + (wy + below)
         self.di[i] = 1.0 / (total + (self.wx[i] + self.wx[i + 1]))
 
@@ -110,13 +127,13 @@
         own = v(i)
         fz = self.wz[i] * (own - pltpu.roll(own, self.lanes - 1, 1))
         result = self.al[i] * own + (fz - pltpu.roll(fz, 1, 1))
-        over = vy[1, i : i + 1, :] if vy is not None else 0.0
+        over = vy[1, pl.ds(i, 1), :] if vy is not None else 0.0
         up = jnp.where(row == self.ny - 1, over, pltpu.roll(own, self.ny - 1, 0))
         fy = self.wy[i] * (own - up)
-        low = self.wl[i : i + 1, :] * ((vy[0, i : i + 1, :] if vy is not None else 0.0) - own[0:1])
+        low = self.wl[pl.ds(i, 1), :] * ((vy[0, pl.ds(i, 1), :] if vy is not None else 0.0) - own[0:1])
         result = result + (fy - jnp.where(row == 0, low, pltpu.roll(fy, 1, 0)))
         for face, j, side in ((i, i - 1, 0), (i + 1, i + 1, 1)):
-            if 0 <= j < self.nx:
+            if not isinstance(i, int) or 0 <= j < self.nx:
                 result = result + self.wx[face] * (own - v(j))
             elif vx is not None:
                 result = result + self.wx[face] * (own - vx[side])
@@ -224,8 +241,8 @@
 
     def pack(e, i, value):
         n = value.shape[0]
-        py[e][0, i : i + 1, :] = value[0:1]
-        py[e][1, i : i + 1, :] = value[n - 1 : n]
+        py[e][0, pl.ds(i, 1), :] = value[0:1]
+        py[e][1, pl.ds(i, 1), :] = value[n - 1 : n]
 
     def put_y(e):
         put(e, 2, py[e].at[0])
@@ -358,7 +375,7 @@
     krows = gather_rows(*kargs)
 
     top = levels[0]
-    inner, outer = list(range(1, nx - 1)), [0, nx - 1]
+    outer = [0, nx - 1]
     k = lambda i: k_ref[i]
     v0 = lambda i: v0_ref[i]
     d0, v1 = s["d0"], s["v1"]
@@ -377,8 +394,7 @@
         v1[i] = v
         pack(E0, i, v)
 
-    for i in inner:
-        first(i)
+    pl.loop(1, nx - 1)(first)
     get(K0, (0, 1))
     get(V0, (0, 1))
     top.x_faces(k, hx[K0])
@@ -457,11 +473,16 @@
             value = value + jnp.where(row == 0, hy[e][0, i : i + 1, :], 0.0)
             into[i] = value + jnp.where(row == n - 1, hy[e][1, i : i + 1, :], 0.0)
 
-    for i in inner:
+    @pl.loop(1, nx - 1)
+    def _(i):
         second(top, i, f0, v1at, d0at, E0, fine)
+
     middle_pairs = tuple(range(1, nx // 2 - 1))
-    for pair in middle_pairs:
+
+    @pl.loop(1, nx // 2 - 1)
+    def _(pair):
         left_over(top, f0, fine, pair, s01, s["fold0"], s["f1"])
+
     get(E0, (0, 1))
     for i in outer:
         second(top, i, f0, v1at, d0at, E0, fine)
@@ -582,11 +603,19 @@
 
 
 def write_out(*refs):
-    sem = refs[8]
-    copies = [pltpu.make_async_copy(refs[t], refs[4 + t], sem.at[t]) for t in range(4)]
-    for one in copies:
+    sources, targets, held, into, out = refs[0:4], refs[4:8], refs[8:12], refs[12], refs[13]
+    pieces = []
+    for t in range(4):
+        for i in range(sources[t].shape[0]):
+            pieces.append((sources[t].at[i], held[t].at[i], targets[t].at[i]))
+    loads = [pltpu.make_async_copy(a, b, into.at[j]) for j, (a, b, _) in enumerate(pieces)]
+    stores = [pltpu.make_async_copy(b, c, out.at[j]) for j, (_, b, c) in enumerate(pieces)]
+    for one in loads:
         one.start()
-    for one in copies:
+    for load, store in zip(loads, stores):
+        load.wait()
+        store.start()
+    for one in stores:
         one.wait()
 
 
@@ -633,7 +662,8 @@
         out_shape=[block(0), block(1), block(2), block(3)],
         in_specs=[anywhere] * 4,
         out_specs=[anywhere] * 4,
-        scratch_shapes=[dma(4)],
+        scratch_shapes=[vm(nx >> l, ny >> l, nz >> l) for l in range(4)]
+        + [dma(sum(nx >> l for l in range(4)))] * 2,
         compiler_params=pltpu.CompilerParams(vmem_limit_bytes=56 * 1024 * 1024),
     )(*fields)
 

time: 62.7 us -> 45.1 us (0.72)
  Pallas kernels: 61.9 us -> 44.3 us
    pallas_call x1, Pallas kernels: 19.6 us -> 1.97 us  [per_device(): pl.pallas_call(write_out, out_shape=[block(0), block(1), block(2), block(...]
where the time goes in v3:
time: 45.1 us; the launch traced here: 44.9 us
  Pallas kernels  44.3 us (98%)
  between operations  0.64 us (1%)
    pallas_call x1, Pallas kernels, per_device(): pl.pallas_call(functools.partial(kernel, nxb, nyb), out_shape=[block(0),...  42.3 us
    pallas_call x1, Pallas kernels, per_device(): pl.pallas_call(write_out, out_shape=[block(0), block(1), block(2), block(...  1.97 us

profile of v3, /device:TPU:0, one launch (start us, length us, event | category | flops | bytes accessed | tf_op | source)
XLA Modules:
  0.0 44.9 jit_solution(14450227653298838600)
XLA Ops:
  0.6 42.3 %shard_map.66 = (f32[8,64,256]{2,1,0:T(8,128)}, f32[4,32,128]{2,1,0:T(8,128)}, f32[2,16,64]{2,1,0:T(8,128)}, f32[1,8,32]{2,1,0:T(8,128)}) custom-call(f32[8,64,256]{2,1,0:T(8,128)} %v0_hbm.1, f32[8,64,256]{2,1,0:T(8,128)} %f_hbm.1, f32[8,64,256]{2,1,0:T(8,128)} %k_hbm.1), custom_call_target="tpu_custom_call" | custom-call | tf_op jit(solution)/shard_map/pallas_call | solution.py:650
  42.9 2.0 %shard_map.67 = (f32[8,64,256]{2,1,0:T(8,128)}, f32[4,32,128]{2,1,0:T(8,128)}, f32[2,16,64]{2,1,0:T(8,128)}, f32[1,8,32]{2,1,0:T(8,128)}) custom-call(f32[8,64,256]{2,1,0:T(8,128)} %get-tuple-element.8.refs_0_, f32[4,32,128]{2,1,0:T(8,128)} %get-tuple-element.9.refs_1_, f32[2,16,64]{2,1,0:T(8,128)} %get-tuple-element.10.refs_2_, ...), custom_call_target="tpu_custom_call" | custom-call | tf_op jit(solution)/shard_map/pallas_call | solution.py:660

commit v4 on v3

--- a/solution.py
+++ b/solution.py
@@ -215,11 +215,6 @@
         made = copy(e, side, src)
         pl.when(has[side])(made.start)
         started.append((made, side))
-        away = (hx if side < 2 else hy)[e]
-
-        @pl.when(jnp.logical_not(has[side]))
-        def _():
-            away[side % 2] = jnp.zeros(away.shape[1:], jnp.float32)
 
     def get(e, sides):
         for side in sides:
@@ -359,6 +354,11 @@
     for i in range(nx):
         pack(V0, i, v0_ref[i])
     put_y(V0)
+    for side in range(4):
+        @pl.when(jnp.logical_not(has[side]))
+        def _():
+            for away in hx if side < 2 else hy:
+                away[side % 2] = jnp.zeros(away.shape[1:], jnp.float32)
 
     restrict([k_ref[i] for i in range(nx)], s01, s["fold0"], s["k1"])
     put_x(K1, s["k1"])
@@ -571,10 +571,28 @@
         ]
 
     image = sum(operate([jnp.ones(shape, jnp.float32)] * low3))
+
+    def left(rows):
+        for made, step_x in rows:
+            if step_x == 0:
+                made.wait_send()
+            else:
+                pl.when(has[0 if step_x < 0 else 1])(made.wait_send)
+
+    for side in range(4):
+        @pl.when(has[side])
+        def _():
+            for made, toward in started:
+                if toward == side:
+                    made.wait_send()
+    left(krows)
+    for made in kcolumns:
+        made.wait_send()
     s["mine"][...] = gathered_rows(*fargs)
     fcargs = (s["mine"], s["whole"], s["wsend"], s["wrecv"])
     fcolumns = gather_columns(*fcargs)
     image = jnp.sum(image)
+    left(frows)
     gathered_columns(*fcargs)
     fc = [s["whole"][:, r, :] for r in range(low3)]
     v = [step[r] * fc[r] for r in range(low3)]
@@ -591,14 +609,7 @@
 
     for one in stores:
         one.wait()
-    for made, side in started:
-        pl.when(has[side])(made.wait_send)
-    for made, step_x in krows + frows:
-        if step_x == 0:
-            made.wait_send()
-        else:
-            pl.when(has[0 if step_x < 0 else 1])(made.wait_send)
-    for made in kcolumns + fcolumns:
+    for made in fcolumns:
         made.wait_send()
 
 

time: 45.1 us -> 45 us (level)
  no operation moved by 1% of the time
where the time goes in v4:
time: 45 us; the launch traced here: 44.8 us
  Pallas kernels  44.2 us (98%)
  between operations  0.64 us (1%)
    pallas_call x1, Pallas kernels, per_device(): pl.pallas_call(functools.partial(kernel, nxb, nyb), out_shape=[block(0),...  42.2 us
    pallas_call x1, Pallas kernels, per_device(): pl.pallas_call(write_out, out_shape=[block(0), block(1), block(2), block(...  1.97 us

profile of v4, /device:TPU:0, one launch (start us, length us, event | category | flops | bytes accessed | tf_op | source)
XLA Modules:
  0.0 44.8 jit_solution(12049890378771981227)
XLA Ops:
  0.6 42.2 %shard_map.66 = (f32[8,64,256]{2,1,0:T(8,128)}, f32[4,32,128]{2,1,0:T(8,128)}, f32[2,16,64]{2,1,0:T(8,128)}, f32[1,8,32]{2,1,0:T(8,128)}) custom-call(f32[8,64,256]{2,1,0:T(8,128)} %v0_hbm.1, f32[8,64,256]{2,1,0:T(8,128)} %f_hbm.1, f32[8,64,256]{2,1,0:T(8,128)} %k_hbm.1), custom_call_target="tpu_custom_call" | custom-call | tf_op jit(solution)/shard_map/pallas_call | solution.py:661
  42.9 2.0 %shard_map.67 = (f32[8,64,256]{2,1,0:T(8,128)}, f32[4,32,128]{2,1,0:T(8,128)}, f32[2,16,64]{2,1,0:T(8,128)}, f32[1,8,32]{2,1,0:T(8,128)}) custom-call(f32[8,64,256]{2,1,0:T(8,128)} %get-tuple-element.8.refs_0_, f32[4,32,128]{2,1,0:T(8,128)} %get-tuple-element.9.refs_1_, f32[2,16,64]{2,1,0:T(8,128)} %get-tuple-element.10.refs_2_, ...), custom_call_target="tpu_custom_call" | custom-call | tf_op jit(solution)/shard_map/pallas_call | solution.py:671
